TPU v7x, 32 devices: a whole 2x2x4 slice. The times are simulated.
32 devices in a mesh: dp: 16 (over z, x, core), section: 2 (over y).
Axes of the slice: x: 2, y: 2, z: 4, core: 2. Of those that a mesh axis runs over, the one named last changes fastest.
Arguments:
- inputs: bfloat16 [2, 2048, 768], P(None, 'dp'), may hold values from -6 to 6
- cotangent: bfloat16 [2, 2048, 768], P(None, 'dp'), may hold values from -6 to 6
- lengths: int32 [2, 16, 3], P(None, 'dp'), may hold values from 1 to 32, 64 in all within a row
- gain_one: float32 [2, 768], P('section'), may hold values from 0.5 to 1.5
- w_qkv: bfloat16 [2, 768, 2304], P('section'), may hold values from -0.21875 to 0.21875
- w_out: bfloat16 [2, 768, 768], P('section'), may hold values from -0.625 to 0.625
- gain_two: float32 [2, 768], P('section'), may hold values from 0.5 to 1.5
- w_up: bfloat16 [2, 768, 3072], P('section'), may hold values from -0.21875 to 0.21875
- b_up: float32 [2, 3072], P('section'), may hold values from -2 to 2
- w_down: bfloat16 [2, 3072, 768], P('section'), may hold values from -0.109375 to 0.109375
- b_down: float32 [2, 768], P('section'), may hold values from -2 to 2
Outputs:
- section_out: bfloat16 [2, 2, 2048, 768], P('section', None, 'dp')
- section_grad: bfloat16 [2, 2, 2048, 768], P('section', None, 'dp')
- grad_gain_one: float32 [2, 768], P('section', 'dp')
- grad_qkv: float32 [2, 768, 2304], P('section', 'dp')
- grad_out: float32 [2, 768, 768], P('section', 'dp')
- grad_gain_two: float32 [2, 768], P('section', 'dp')
- grad_up: float32 [2, 768, 3072], P('section', 'dp')
- grad_bias_up: float32 [2, 3072], P('section', 'dp')
- grad_down: float32 [2, 3072, 768], P('section', 'dp')
- grad_bias_down: float32 [2, 768], P('section', 'dp')
Inputs may be any that keep to these rules, and one draw needn't show every extreme that they name: Each row of 3 entries sums to 64: the first 2 are the lengths of the slot's documents in order, the last the padding rows at its end.
All inputs are finite; a program needn't handle non-finite values.
Results may differ from a plain program's by a relative error of at most 0.015.
Values may be sent and summed in bfloat16 or wider, within the bound.
A program may use at most 320 MiB of HBM per device.

v0:
```python
from functools import partial
import math

import jax
import jax.numpy as jnp
from jax import lax
from jax.sharding import PartitionSpec as P

D = 768
FF = 3072
HEADS = 12
HEAD_DIM = 64
BLOCK = 16
SEGS = 3
SEQ_TOK = 64


EPSILON = 1e-05


def passed_along(block, axis, distance):
    devices = range(lax.axis_size(axis))
    route = [(i - distance, i) for i in devices if i - distance in devices]
    return lax.ppermute(block, axis, route)


def row_tables(lengths_row):
    steps_all = jnp.arange(SEQ_TOK, dtype=jnp.int32)
    bounds = jnp.cumsum(lengths_row)
    passed = (steps_all[:, None] >= bounds[None, :]).astype(jnp.int32)
    document = jnp.sum(passed, axis=1)
    offset = jnp.sum(passed * lengths_row[None, :], axis=1)
    position = steps_all - offset
    inside = document < SEGS - 1
    document_rows = jnp.concatenate([document, document])
    position_rows = jnp.concatenate([position, position])
    inside_rows = jnp.concatenate([inside, inside])
    copies = jnp.concatenate([jnp.zeros((SEQ_TOK,), jnp.int32), jnp.ones((SEQ_TOK,), jnp.int32)])
    blocks = position_rows // BLOCK
    query_block = blocks[:, None]
    key_block = blocks[None, :]
    noisy_query = (copies == 0)[:, None]
    noisy_key = (copies == 0)[None, :]
    ruling = jnp.where(
        noisy_query,
        jnp.where(noisy_key, key_block == query_block, key_block < query_block),
        jnp.logical_and(jnp.logical_not(noisy_key), key_block <= query_block),
    )
    same_doc = (
        (document_rows[:, None] == document_rows[None, :])
        & inside_rows[:, None]
        & inside_rows[None, :]
    )
    indices = jnp.arange(2 * SEQ_TOK, dtype=jnp.int32)
    allowed = same_doc & ruling | (indices[:, None] == indices[None, :])
    frequency = jnp.exp(
        jnp.arange(HEAD_DIM // 2).astype(jnp.float32) * (-2.0 * math.log(10000.0) / HEAD_DIM)
    )
    angles = position_rows.astype(jnp.float32)[:, None] * frequency[None, :]
    return (allowed, jnp.cos(angles), jnp.sin(angles))


def rotate(tensor, cosine, sine):
    halfway = tensor.shape[-1] // 2
    upper_part = tensor[..., :halfway]
    lower_part = tensor[..., halfway:]
    cos_rows = cosine[:, None, :]
    sin_rows = sine[:, None, :]
    return jnp.concatenate(
        [
            upper_part * cos_rows - lower_part * sin_rows,
            upper_part * sin_rows + lower_part * cos_rows,
        ],
        axis=-1,
    )


def unrotate(gradient, cosine, sine):
    halfway = gradient.shape[-1] // 2
    upper_part = gradient[..., :halfway]
    lower_part = gradient[..., halfway:]
    cos_rows = cosine[:, None, :]
    sin_rows = sine[:, None, :]
    return jnp.concatenate(
        [
            upper_part * cos_rows + lower_part * sin_rows,
            lower_part * cos_rows - upper_part * sin_rows,
        ],
        axis=-1,
    )


def normalize(values):
    centred = values - jnp.mean(values, axis=-1, keepdims=True)
    inverse = lax.rsqrt(jnp.mean(centred * centred, axis=-1, keepdims=True) + EPSILON)
    return (centred * inverse, inverse)


def normal_back(d_normed, normed, inverse):
    return inverse * (
        d_normed
        - jnp.mean(d_normed, axis=-1, keepdims=True)
        - normed * jnp.mean(d_normed * normed, axis=-1, keepdims=True)
    )


def scores_of(query, keyset, allowed):
    raw = jnp.einsum(
        "qhd,khd->hqk", query, keyset, preferred_element_type=jnp.float32
    ) * HEAD_DIM ** (-0.5)
    return jnp.where(allowed[None], raw, -1e30)


def forward_pass(state, lengths_row, weights):
    gain_a, w_qkv, w_out, gain_b, w_up, b_up, w_down, b_down = weights
    allowed, cosine, sine = row_tables(lengths_row)
    count = state.shape[0]
    widened = state.astype(jnp.float32)
    normed, inverse = normalize(widened)
    entry = (normed * gain_a).astype(jnp.bfloat16)
    joined = jnp.dot(entry, w_qkv, preferred_element_type=jnp.float32)
    query = rotate(joined[:, :D].reshape(count, HEADS, HEAD_DIM), cosine, sine).astype(jnp.bfloat16)
    keyset = rotate(joined[:, D : 2 * D].reshape(count, HEADS, HEAD_DIM), cosine, sine).astype(
        jnp.bfloat16
    )
    valueset = joined[:, 2 * D :].reshape(count, HEADS, HEAD_DIM).astype(jnp.bfloat16)
    scores = scores_of(query, keyset, allowed)
    highest = jnp.max(scores, axis=-1, keepdims=True)
    exponent = jnp.exp(scores - highest)
    totals = jnp.sum(exponent, axis=-1, keepdims=True)
    soft_low = (exponent / totals).astype(jnp.bfloat16)
    log_total = highest + jnp.log(totals)
    mixed = (
        jnp.einsum("hqk,khd->qhd", soft_low, valueset, preferred_element_type=jnp.float32)
        .reshape(count, D)
        .astype(jnp.bfloat16)
    )
    hidden = widened + jnp.dot(mixed, w_out, preferred_element_type=jnp.float32)
    normed_two, inverse_two = normalize(hidden)
    entry_two = (normed_two * gain_b).astype(jnp.bfloat16)
    inner = jnp.dot(entry_two, w_up, preferred_element_type=jnp.float32) + b_up
    activated = jax.nn.gelu(inner, approximate=True).astype(jnp.bfloat16)
    result = (
        hidden + jnp.dot(activated, w_down, preferred_element_type=jnp.float32) + b_down
    ).astype(jnp.bfloat16)
    saved = (
        normed,
        inverse,
        entry,
        query,
        keyset,
        valueset,
        log_total,
        mixed,
        normed_two,
        inverse_two,
        entry_two,
        inner,
        activated,
    )
    return (result, saved)


def forward_blank(state, lengths_row, weights):
    count = state.shape[0]
    rows_f = jnp.zeros((count, D), jnp.float32)
    rows_b = jnp.zeros((count, D), jnp.bfloat16)
    column = jnp.zeros((count, 1), jnp.float32)
    heads_b = jnp.zeros((count, HEADS, HEAD_DIM), jnp.bfloat16)
    saved = (
        rows_f,
        column,
        rows_b,
        heads_b,
        heads_b,
        heads_b,
        jnp.zeros((HEADS, count, 1), jnp.float32),
        rows_b,
        rows_f,
        column,
        rows_b,
        jnp.zeros((count, FF), jnp.float32),
        jnp.zeros((count, FF), jnp.bfloat16),
    )
    return (jnp.zeros_like(state), saved)


def settle_plain(index, group):
    return group


def backward_core(saved, incoming, lengths_row, weights, settle):
    gain_a, w_qkv, w_out, gain_b, w_up, b_up, w_down, b_down = weights
    (
        normed,
        inverse,
        entry,
        query,
        keyset,
        valueset,
        log_total,
        mixed,
        normed_two,
        inverse_two,
        entry_two,
        inner,
        activated,
    ) = saved
    allowed, cosine, sine = row_tables(lengths_row)
    count = incoming.shape[0]
    upper = incoming.astype(jnp.float32)
    grad_down = jnp.einsum("rf,rd->fd", activated, incoming, preferred_element_type=jnp.float32)
    grad_bias_down = jnp.sum(upper, axis=0)
    d_activated = jnp.einsum("rd,fd->rf", incoming, w_down, preferred_element_type=jnp.float32)
    _, gelu_pull = jax.vjp(partial(jax.nn.gelu, approximate=True), inner)
    d_inner = gelu_pull(d_activated)[0].astype(jnp.bfloat16)
    grad_up = jnp.einsum("rd,rf->df", entry_two, d_inner, preferred_element_type=jnp.float32)
    grad_bias_up = jnp.sum(d_inner, axis=0, dtype=jnp.float32)
    d_entry_two = jnp.einsum("rf,df->rd", d_inner, w_up, preferred_element_type=jnp.float32)
    grad_gain_b = jnp.sum(d_entry_two * normed_two, axis=0)
    feed_group = settle(0, (grad_gain_b, grad_up, grad_bias_up, grad_down, grad_bias_down))
    d_hidden = upper + normal_back(d_entry_two * gain_b, normed_two, inverse_two)
    d_branch = d_hidden.astype(jnp.bfloat16)
    grad_out = jnp.einsum("rd,re->de", mixed, d_branch, preferred_element_type=jnp.float32)
    d_mixed = (
        jnp.einsum("re,de->rd", d_branch, w_out, preferred_element_type=jnp.float32)
        .astype(jnp.bfloat16)
        .reshape(count, HEADS, HEAD_DIM)
    )
    scores = scores_of(query, keyset, allowed)
    probs = jnp.exp(scores - log_total)
    d_probs = jnp.einsum("qhd,khd->hqk", d_mixed, valueset, preferred_element_type=jnp.float32)
    d_scores = (probs * (d_probs - jnp.sum(probs * d_probs, axis=-1, keepdims=True))).astype(
        jnp.bfloat16
    )
    d_values = jnp.einsum(
        "hqk,qhd->khd", probs.astype(jnp.bfloat16), d_mixed, preferred_element_type=jnp.float32
    )
    scaling = HEAD_DIM ** (-0.5)
    d_query = (
        jnp.einsum("hqk,khd->qhd", d_scores, keyset, preferred_element_type=jnp.float32) * scaling
    )
    d_keys = (
        jnp.einsum("hqk,qhd->khd", d_scores, query, preferred_element_type=jnp.float32) * scaling
    )
    d_joined = jnp.concatenate(
        [
            unrotate(d_query, cosine, sine).reshape(count, D),
            unrotate(d_keys, cosine, sine).reshape(count, D),
            d_values.reshape(count, D),
        ],
        axis=1,
    ).astype(jnp.bfloat16)
    grad_qkv = jnp.einsum("rd,re->de", entry, d_joined, preferred_element_type=jnp.float32)
    d_entry = jnp.einsum("re,de->rd", d_joined, w_qkv, preferred_element_type=jnp.float32)
    grad_gain_a = jnp.sum(d_entry * normed, axis=0)
    attn_group = settle(1, (grad_gain_a, grad_qkv, grad_out))
    d_state = (d_hidden + normal_back(d_entry * gain_a, normed, inverse)).astype(jnp.bfloat16)
    return (d_state, tuple(attn_group) + tuple(feed_group))


def backward_pass(saved, incoming, lengths_row, weights):
    return backward_core(saved, incoming, lengths_row, weights, settle_plain)


def backward_blank(saved, incoming, lengths_row, weights):
    return (
        jnp.zeros_like(incoming),
        tuple((jnp.zeros(item.shape, jnp.float32) for item in weights)),
    )


def keep_at(place, active, stack, leaf):
    current = lax.dynamic_index_in_dim(stack, place, 0, keepdims=False)
    return lax.dynamic_update_index_in_dim(stack, jnp.where(active, leaf, current), place, 0)


def reduce_total(grads):
    (
        grad_gain_a,
        grad_qkv,
        grad_out,
        grad_gain_b,
        grad_up,
        grad_bias_up,
        grad_down,
        grad_bias_down,
    ) = grads
    return (
        lax.psum_scatter(grad_gain_a[None], "dp", scatter_dimension=1, tiled=True),
        lax.psum_scatter(grad_qkv[None], "dp", scatter_dimension=1, tiled=True),
        lax.psum_scatter(grad_out[None], "dp", scatter_dimension=1, tiled=True),
        lax.psum_scatter(grad_gain_b[None], "dp", scatter_dimension=1, tiled=True),
        lax.psum_scatter(grad_up[None], "dp", scatter_dimension=1, tiled=True),
        lax.psum_scatter(grad_bias_up[None], "dp", scatter_dimension=1, tiled=True),
        lax.psum_scatter(grad_down[None], "dp", scatter_dimension=1, tiled=True),
        lax.psum_scatter(grad_bias_down[None], "dp", scatter_dimension=1, tiled=True),
    )


def on_device(
    inputs, cotangent, lengths, gain_one, w_qkv, w_out, gain_two, w_up, b_up, w_down, b_down
):
    section = lax.axis_index("section")
    micro = inputs.shape[0]
    weights = (gain_one[0], w_qkv[0], w_out[0], gain_two[0], w_up[0], b_up[0], w_down[0], b_down[0])
    slot_lengths = lengths[:, 0]
    arrived = jnp.zeros(inputs.shape[1:], jnp.bfloat16)
    results = jnp.zeros(inputs.shape, jnp.bfloat16)
    stored = ()
    for tick in range(micro + 1):
        number = tick - section
        active = jnp.logical_and(number >= 0, number < micro)
        place = jnp.clip(number, 0, micro - 1)
        layer_in = jnp.where(section == 0, inputs[min(tick, micro - 1)], arrived)
        lengths_row = lax.dynamic_index_in_dim(slot_lengths, place, 0, keepdims=False)
        result, saved = lax.cond(
            active, forward_pass, forward_blank, layer_in, lengths_row, weights
        )
        if tick == 0:
            stored = jax.tree.map(lambda leaf: jnp.zeros((micro,) + leaf.shape, leaf.dtype), saved)
        stored = jax.tree.map(partial(keep_at, place, active), stored, saved)
        results = keep_at(place, active, results, result)
        if tick < micro:
            arrived = passed_along(result, "section", 1)
    back_arrived = jnp.zeros(inputs.shape[1:], jnp.bfloat16)
    grads_in = jnp.zeros(inputs.shape, jnp.bfloat16)
    totals = tuple((jnp.zeros(item.shape, jnp.float32) for item in weights))
    reduced_sums = ()
    for tick in range(micro + 1):
        number = tick - (1 - section)
        active = jnp.logical_and(number >= 0, number < micro)
        place = jnp.clip(number, 0, micro - 1)
        incoming = jnp.where(section == 1, cotangent[min(tick, micro - 1)], back_arrived)
        saved = jax.tree.map(
            lambda stack: lax.dynamic_index_in_dim(stack, place, 0, keepdims=False), stored
        )
        lengths_row = lax.dynamic_index_in_dim(slot_lengths, place, 0, keepdims=False)
        d_state, grads = lax.cond(
            active, backward_pass, backward_blank, saved, incoming, lengths_row, weights
        )
        totals = tuple((earlier + later for earlier, later in zip(totals, grads)))
        grads_in = keep_at(place, active, grads_in, d_state)
        if tick < micro:
            back_arrived = passed_along(d_state, "section", -1)
    reduced_sums = reduce_total(totals)
    sum_gain_a, sum_qkv, sum_out, sum_gain_b, sum_up, sum_bias_up, sum_down, sum_bias_down = (
        reduced_sums
    )
    return (
        results[None],
        grads_in[None],
        sum_gain_a,
        sum_qkv,
        sum_out,
        sum_gain_b,
        sum_up,
        sum_bias_up,
        sum_down,
        sum_bias_down,
    )


def solution(mesh):
    placed = (
        P(None, "dp", None),
        P(None, "dp", None),
        P(None, "dp", None),
        P("section", None),
        P("section", None, None),
        P("section", None, None),
        P("section", None),
        P("section", None, None),
        P("section", None),
        P("section", None, None),
        P("section", None),
    )
    return jax.shard_map(
        on_device,
        mesh=mesh,
        in_specs=placed,
        out_specs=(
            P("section", None, "dp", None),
            P("section", None, "dp", None),
            P("section", "dp"),
            P("section", "dp", None),
            P("section", "dp", None),
            P("section", "dp"),
            P("section", "dp", None),
            P("section", "dp"),
            P("section", "dp", None),
            P("section", "dp"),
        ),
        check_vma=False,
    )
```

profile of v0, /device:TPU:0, one launch (start us, length us, event | category | flops | bytes accessed | tf_op | source)
XLA Modules:
  0.0 981.5 jit_solution(17963686984438412557)
XLA Ops:
  8.0 20.7 %conditional.6 = (bf16[128,768]{1,0:T(8,128)(2,1)}, f32[128,768]{1,0:T(8,128)S(1)}, f32[128,1]{0,1:T(1,128)}, bf16[128,768]{1,0:T(8,128)(2,1)S(1)}, bf16[128,12,...) conditional(s32[]{:T(128)} %convert_element_type.405, () %tuple.74, ...), branch_computations={%region_0.1_spmd, %region_1.11_spmd} | conditional | flops 1872107648 | bytes 59727036 | solution.py:317
  15.1 2.7 fusion.295
  21.2 4.7 fusion.7
  25.9 2.7 fusion.10
  28.7 2.1 collective-permute-start
  30.9 1.6 slice_bitcast_fusion.1
  49.5 45.7 %conditional.7 = (bf16[128,768]{1,0:T(8,128)(2,1)}, f32[128,768]{1,0:T(8,128)}, f32[128,1]{0,1:T(1,128)}, bf16[128,768]{1,0:T(8,128)(2,1)}, bf16[128,12,64]{0,2,...) conditional(s32[]{:T(128)} %convert_element_type.406, () %tuple.76, ...), branch_computations={%region_11.12_spmd, %region_12.22_spmd} | conditional | flops 1872107648 | bytes 48022576 | solution.py:317
  60.9 1.5 fusion.36
  63.8 1.9 multiply_convert_fusion.3
  65.7 2.8 fusion.296
  70.2 2.0 copy.134
  72.1 1.8 copy.132
  73.9 1.9 copy.133
  79.4 1.9 convolution_convert_fusion.1
  81.9 1.7 copy.179
  86.8 5.6 fusion.28
  92.5 2.6 fusion.31
  98.7 1.8 bitcast_dynamic-update-slice_fusion.31
  100.5 1.6 constant_dynamic-slice_fusion.29
  102.1 2.2 bitcast_dynamic-update-slice_fusion.25
  104.3 1.6 constant_dynamic-slice_fusion.23
  105.9 1.6 constant_dynamic-slice_fusion.27
  116.3 1.5 bitcast_dynamic-update-slice_fusion.4
  118.8 1.7 bitcast_dynamic-update-slice_fusion.1
  123.3 10.7 %conditional.8 = (bf16[128,768]{1,0:T(8,128)(2,1)}, f32[128,768]{1,0:T(8,128)}, f32[128,1]{0,1:T(1,128)}, bf16[128,768]{1,0:T(8,128)(2,1)}, bf16[128,12,64]{0,2,...) conditional(s32[]{:T(128)} %convert_element_type.407, () %tuple.78, ...), branch_computations={%region_22.23_spmd, %region_23.33_spmd} | conditional | flops 1872107648 | bytes 48022576 | solution.py:317
  134.1 1.5 bitcast_dynamic-update-slice_fusion.3
  140.8 2.8 copy-done
  144.2 8.1 conditional.9
  147.2 4.7 broadcast.2236
  152.4 8.8 collective-permute-start.2
  162.1 70.4 %collective-permute-done.2 = bf16[128,768]{1,0:T(8,128)(2,1)S(1)} collective-permute-done((bf16[128,768]{1,0:T(8,128)(2,1)S(1)}, bf16[128,768]{1,0:T(8,128)(2,1)S(1)}, u32[]{:S(2)}, u32[]{:S(2)}) %collective-permute-start.2) | collective-permute-done | bytes 196640 | tf_op jit(solution)/shard_map/ppermute | solution.py:24
  232.6 52.9 %conditional.10 = (bf16[128,768]{1,0:T(8,128)(2,1)}, f32[768]{0:T(1024)}, f32[768,2304]{1,0:T(8,128)}, f32[768,768]{1,0:T(8,128)}, f32[768]{0:T(1024)}, /*index=...) conditional(s32[]{:T(128)} %convert_element_type.409, () %tuple.82, ...), branch_computations={%region_47.48_spmd, %region_48.61_spmd} | conditional | flops 3768877568 | bytes 100929608 | solution.py:339
  232.6 1.6 convert_reduce_fusion.10
  234.1 6.4 convert_reduce_fusion.9
  251.6 5.0 fusion.156
  258.7 1.7 copy.145
  266.4 1.9 fusion.152
  269.2 1.9 fusion.162
  271.2 4.1 fusion.158
  275.3 5.1 fusion.144
  280.4 5.0 fusion.160
  286.7 7.0 collective-permute-done.3
  293.7 51.6 %conditional.11 = (bf16[128,768]{1,0:T(8,128)(2,1)}, f32[768]{0:T(1024)}, f32[768,2304]{1,0:T(8,128)}, f32[768,768]{1,0:T(8,128)}, f32[768]{0:T(1024)}, /*index=...) conditional(s32[]{:T(128)} %convert_element_type.410, () %tuple.84, ...), branch_computations={%region_61.62_spmd, %region_62.75_spmd} | conditional | flops 3768877568 | bytes 101740680 | solution.py:339
  293.9 1.8 convert_reduce_fusion.13
  295.7 6.4 convert_reduce_fusion.12
  313.1 5.0 fusion.223
  326.6 1.9 fusion.219
  329.3 1.9 fusion.229
  331.3 4.0 fusion.225
  335.3 5.0 fusion.211
  340.3 5.1 fusion.227
  351.2 1.6 copy.172
  353.3 4.3 add_bitcast_fusion.6
  357.9 11.4 %add_bitcast_fusion.5 = f32[1,768,2304]{2,1,0:T(8,128)} fusion(f32[768,2304]{1,0:T(8,128)} %get-tuple-element.1096, f32[768,2304]{1,0:T(8,128)} %copy-done.7, f32[768,2304]{1,0:T(8,128)} %get-tuple-element.1095), kind=kLoop, calls=%fused_computation.553 | loop fusion | flops 3538944 | bytes 28311552 | tf_op jit(solution)/shard_map/broadcast_in_dim | solution.py:291
  369.4 14.8 %add_bitcast_fusion.4 = f32[1,768,3072]{2,1,0:T(8,128)} fusion(f32[768,3072]{1,0:T(8,128)} %get-tuple-element.1105, f32[768,3072]{1,0:T(8,128)} %get-tuple-element.1103, f32[768,3072]{1,0:T(8,128)} %get-tuple-element.1104), kind=kLoop, calls=%fused_computation.552 | loop fusion | flops 4718592 | bytes 37748736 | tf_op jit(solution)/shard_map/broadcast_in_dim | solution.py:294
  384.3 13.9 %add_bitcast_fusion.3 = f32[1,3072,768]{2,1,0:T(8,128)} fusion(f32[3072,768]{1,0:T(8,128)} %get-tuple-element.1111, f32[3072,768]{1,0:T(8,128)} %copy-done.3, f32[3072,768]{1,0:T(8,128)} %get-tuple-element.1110), kind=kLoop, calls=%fused_computation.551 | loop fusion | flops 4718592 | bytes 37748736 | tf_op jit(solution)/shard_map/broadcast_in_dim | solution.py:296
  404.2 57.2 %reduce-scatter.27.cloned.1.call-done = f32[48,1]{1,0:T(8,128)} async-done(((f32[768,1]{1,0:T(8,128)}), f32[48,1]{1,0:T(8,128)}) %reduce-scatter.27.cloned.1.call-update) | async-done | bytes 208
  462.7 56.8 %reduce-scatter.31.cloned.1.call-done = f32[48,1]{1,0:T(8,128)} async-done(((f32[768,1]{1,0:T(8,128)}), f32[48,1]{1,0:T(8,128)}) %reduce-scatter.31.cloned.1.call-update) | async-done | bytes 208
  520.8 61.2 %reduce-scatter.29.cloned.1.call-done = f32[192,1]{1,0:T(8,128)} async-done(((f32[3072,1]{1,0:T(8,128)}), f32[192,1]{1,0:T(8,128)}) %reduce-scatter.29.cloned.1.call-update) | async-done | bytes 784
  582.0 1.5 copy.173
  583.5 64.7 %reduce-scatter.19.cloned.1.call-done = f32[1,48,768]{2,1,0:T(8,128)} async-done(((f32[1,768,768]{2,1,0:T(8,128)}), f32[1,48,768]{2,1,0:T(8,128)}) %reduce-scatter.19.cloned.1.call-update) | async-done | bytes 147472 | tf_op jit(solution)/shard_map/reduce_scatter | solution.py:292
  648.2 94.1 %reduce-scatter.17.cloned.1.call-done = f32[1,48,2304]{2,1,0:T(8,128)} async-done(((f32[1,768,2304]{2,1,0:T(8,128)}), f32[1,48,2304]{2,1,0:T(8,128)}) %reduce-scatter.17.cloned.1.call-update) | async-done | bytes 442384 | tf_op jit(solution)/shard_map/reduce_scatter | solution.py:291
  742.3 115.6 %reduce-scatter.21.cloned.1.call-done = f32[1,48,3072]{2,1,0:T(8,128)} async-done(((f32[1,768,3072]{2,1,0:T(8,128)}), f32[1,48,3072]{2,1,0:T(8,128)}) %reduce-scatter.21.cloned.1.call-update) | async-done | bytes 589840 | tf_op jit(solution)/shard_map/reduce_scatter | solution.py:294
  858.0 116.4 %reduce-scatter.23.cloned.1.call-done = f32[1,192,768]{2,1,0:T(8,128)} async-done(((f32[1,3072,768]{2,1,0:T(8,128)}), f32[1,192,768]{2,1,0:T(8,128)}) %reduce-scatter.23.cloned.1.call-update) | async-done | bytes 589840 | tf_op jit(solution)/shard_map/reduce_scatter | solution.py:296
  (579 shorter events, 142.0 us)
Async XLA Ops:
  7.2 395.6 %reduce-scatter.25.cloned.1.call-start = ((), (), s32[]{:S(2)}) async-start(), calls=%async_computation.12 | async-start | bytes 417792
  21.0 4.9 slice-start
  21.1 4.7 copy-start.114
  21.2 4.7 slice-start.1
  28.7 6.7 copy-start.103
  28.7 7.5 copy-start.106
  28.7 7.7 copy-start.31
  28.7 7.7 copy-start.85
  28.7 7.7 copy-start.145
  28.7 20.1 %collective-permute-start = (bf16[128,768]{1,0:T(8,128)(2,1)}, bf16[128,768]{1,0:T(8,128)(2,1)}, u32[]{:S(2)}, u32[]{:S(2)}) collective-permute-start(bf16[128,768]{1,0:T(8,128)(2,1)} %get-tuple-element.1046), channel_id=1, source_target_pairs={{0,1},{2,3},{4,5},{6,7},{8,9},{10,11},{12,13},{14,15},{16,17},{18,... | collective-permute-start | bytes 589832 | tf_op jit(solution)/shard_map/ppermute | solution.py:24
  32.5 4.7 copy-start.117
  33.5 14.5 %copy-start.66 = (bf16[2,128,768]{2,1,0:T(8,128)(2,1)}, bf16[2,128,768]{2,1,0:T(8,128)(2,1)S(1)}, u32[]{:S(2)}) copy-start(bf16[2,128,768]{2,1,0:T(8,128)(2,1)S(1)} %bitcast_dynamic-update-slice_fusion.35) | copy-start | bytes 1179652
  85.9 6.6 slice-start.2
  86.8 5.7 slice-start.3
  86.8 5.7 copy-start.155
  95.1 12.4 %copy-start.51 = (bf16[2,128,768]{2,1,0:T(8,128)(2,1)S(1)}, bf16[2,128,768]{2,1,0:T(8,128)(2,1)}, u32[]{:S(2)}) copy-start(bf16[2,128,768]{2,1,0:T(8,128)(2,1)} %copy-done.50) | copy-start | bytes 1179652
  95.1 12.4 %copy-start.127 = (bf16[1,128,768]{2,1,0:T(8,128)(2,1)S(1)}, bf16[1,128,768]{2,1,0:T(8,128)(2,1)}, u32[]{:S(2)}) copy-start(bf16[1,128,768]{2,1,0:T(8,128)(2,1)} %get-tuple-element.1493) | copy-start | bytes 589828
  102.1 7.3 copy-start.40
  102.1 7.3 copy-start.59
  102.1 7.3 copy-start.128
  102.1 7.3 copy-start.129
  107.5 5.8 copy-start.22
  107.5 5.8 copy-start.110
  107.5 5.9 copy-start.111
  108.7 4.7 copy-start.52
  112.0 11.2 %collective-permute-start.1 = (bf16[128,768]{1,0:T(8,128)(2,1)}, bf16[128,768]{1,0:T(8,128)(2,1)S(1)}, u32[]{:S(2)}, u32[]{:S(2)}) collective-permute-start(bf16[128,768]{1,0:T(8,128)(2,1)} %get-tuple-element.1047), channel_id=1, source_target_pairs={{0,1},{2,3},{4,5},{6,7},{8,9},{10,11},{12,13},{14,15},{16,17},{18,... | collective-permute-start | bytes 589832 | tf_op jit(solution)/shard_map/ppermute | solution.py:24
  139.4 4.2 copy-start.164
  152.3 80.2 %copy-start.3 = (f32[3072,768]{1,0:T(8,128)}, f32[3072,768]{1,0:T(8,128)S(1)}, u32[]{:S(2)}) copy-start(f32[3072,768]{1,0:T(8,128)S(1)} %get-tuple-element.1109) | copy-start | bytes 28311556
  152.3 80.2 %copy-start.7 = (f32[768,2304]{1,0:T(8,128)}, f32[768,2304]{1,0:T(8,128)S(1)}, u32[]{:S(2)}) copy-start(f32[768,2304]{1,0:T(8,128)S(1)} %get-tuple-element.1094) | copy-start | bytes 21233668
  152.3 80.2 %copy-start.27 = (f32[768,768]{1,0:T(8,128)}, f32[768,768]{1,0:T(8,128)S(1)}, u32[]{:S(2)}) copy-start(f32[768,768]{1,0:T(8,128)S(1)} %get-tuple-element.1097) | copy-start | bytes 7077892
  152.3 80.2 %copy-start.119 = (bf16[128,768]{1,0:T(8,128)(2,1)}, bf16[128,768]{1,0:T(8,128)(2,1)S(1)}, u32[]{:S(2)}) copy-start(bf16[128,768]{1,0:T(8,128)(2,1)S(1)} %get-tuple-element.1088) | copy-start | bytes 589828
  152.4 80.2 %copy-start.154 = (f32[768]{0:T(1024)}, f32[768]{0:T(1024)S(1)}, u32[]{:S(2)}) copy-start(f32[768]{0:T(1024)S(1)} %get-tuple-element.1091) | copy-start | bytes 9220
  152.4 80.1 %collective-permute-start.2 = (bf16[128,768]{1,0:T(8,128)(2,1)S(1)}, bf16[128,768]{1,0:T(8,128)(2,1)S(1)}, u32[]{:S(2)}, u32[]{:S(2)}) collective-permute-start(bf16[128,768]{1,0:T(8,128)(2,1)S(1)} %get-tuple-element.1088), channel_id=1, source_target_pairs={{1,0},{3,2},{5,4},{7,6},{9,8},{11,10},{13,12},{15,14},{17,16},{19,... | collective-permute-start | bytes 589832 | tf_op jit(solution)/shard_map/ppermute | solution.py:24
  162.1 70.5 %copy-start.95 = (bf16[128,768]{1,0:T(8,128)(2,1)}, bf16[128,768]{1,0:T(8,128)(2,1)S(1)}, u32[]{:S(2)}) copy-start(bf16[128,768]{1,0:T(8,128)(2,1)S(1)} %slice_bitcast_fusion) | copy-start | bytes 589828
  234.1 6.4 copy-start.77
  234.1 7.0 copy-start.165
  234.1 7.0 copy-start.170
  234.1 7.5 copy-start.160
  251.6 5.0 copy-start.78
  251.6 5.0 copy-start.142
  251.6 5.0 copy-start.178
  271.2 4.1 copy-start.79
  275.3 5.1 copy-start.64
  275.3 5.1 copy-start.72
  285.4 8.3 collective-permute-start.3
  295.7 6.4 copy-start.80
  295.7 7.0 copy-start.166
  295.7 7.0 copy-start.171
  295.7 7.5 copy-start.161
  313.1 5.0 copy-start.81
  313.1 5.0 copy-start.143
  313.1 5.0 copy-start.179
  335.3 5.0 copy-start.65
  335.3 5.0 copy-start.73
  345.3 5.1 copy-start.140
  347.0 114.4 %reduce-scatter.27.cloned.1.call-start = ((), (), s32[]{:S(2)}) async-start(), calls=%async_computation.13 | async-start | bytes 417792
  348.7 170.8 %reduce-scatter.31.cloned.1.call-start = ((), (), s32[]{:S(2)}) async-start(), calls=%async_computation.15 | async-start | bytes 417792
  350.4 231.6 %reduce-scatter.29.cloned.1.call-start = ((), (), s32[]{:S(2)}) async-start(), calls=%async_computation.14 | async-start | bytes 1671168
  352.8 295.4 %reduce-scatter.19.cloned.1.call-start = ((), (), s32[]{:S(2)}) async-start(), calls=%async_computation.9 | async-start | bytes 2506752 | tf_op jit(solution)/shard_map/reduce_scatter | solution.py:292
  357.6 384.7 %reduce-scatter.17.cloned.1.call-start = ((), (), s32[]{:S(2)}) async-start(), calls=%async_computation.8 | async-start | bytes 7520256 | tf_op jit(solution)/shard_map/reduce_scatter | solution.py:291
  369.4 488.6 %reduce-scatter.21.cloned.1.call-start = ((), (), s32[]{:S(2)}) async-start(), calls=%async_computation.10 | async-start | bytes 10027008 | tf_op jit(solution)/shard_map/reduce_scatter | solution.py:294
  384.3 590.1 %reduce-scatter.23.cloned.1.call-start = ((), (), s32[]{:S(2)}) async-start(), calls=%async_computation.11 | async-start | bytes 10027008 | tf_op jit(solution)/shard_map/reduce_scatter | solution.py:296
  400.5 573.8 %copy-start.130 = (bf16[1,2,128,768]{3,2,1,0:T(8,128)(2,1)}, bf16[1,2,128,768]{3,2,1,0:T(8,128)(2,1)S(1)}, u32[]{:S(2)}) copy-start(bf16[1,2,128,768]{3,2,1,0:T(8,128)(2,1)S(1)} %bitcast_dynamic-update-slice_fusion.33) | copy-start | bytes 1179652
  402.7 571.7 %copy-start.131 = (bf16[1,2,128,768]{3,2,1,0:T(8,128)(2,1)}, bf16[1,2,128,768]{3,2,1,0:T(8,128)(2,1)S(1)}, u32[]{:S(2)}) copy-start(bf16[1,2,128,768]{3,2,1,0:T(8,128)(2,1)S(1)} %bitcast_dynamic-update-slice_fusion.12) | copy-start | bytes 1179652
  (109 other events, 227.4 us)
Sparse Core Ops, SparseCore 0:
  347.1 55.6 reduce-scatter.24
  406.7 54.6 reduce-scatter.26
  464.8 54.5 reduce-scatter.30
  523.4 58.5 reduce-scatter.28
  586.2 62.0 reduce-scatter.18
  653.2 89.0 reduce-scatter.16
  747.0 110.8 reduce-scatter.20
  863.2 111.1 reduce-scatter.22
where the time goes:
time: 989 us; the launch traced here: 981 us
  waiting for transfers between devices  644 us (65%)
  other arithmetic  123 us (12%)
  matrix products  94.5 us (10%)
  local copies, waits for them, and re-layouts  88.7 us (9%)
  between operations  15.7 us (2%)
  starting transfers between devices  14 us (1%)
    unnamed x12, waiting for transfers between devices  175 us
    reduce_scatter x1, waiting for transfers between devices, reduce_total(): lax.psum_scatter(grad_down[None], 'dp', scatter_dimension=1, tiled=True)  116 us
    reduce_scatter x1, waiting for transfers between devices, reduce_total(): lax.psum_scatter(grad_up[None], 'dp', scatter_dimension=1, tiled=True)  116 us
    reduce_scatter x1, waiting for transfers between devices, reduce_total(): lax.psum_scatter(grad_qkv[None], 'dp', scatter_dimension=1, tiled=True)  94.1 us
    ppermute x4, waiting for transfers between devices, passed_along(): return lax.ppermute(block, axis, route)  77.4 us
    reduce_scatter x1, waiting for transfers between devices, reduce_total(): lax.psum_scatter(grad_out[None], 'dp', scatter_dimension=1, tiled=True)  64.7 us
    dynamic_update_slice x41, other arithmetic, keep_at(): lax.dynamic_update_index_in_dim(stack, jnp.where(active, leaf, current),...  24.7 us
    unnamed x194, local copies, waits for them, and re-layouts  20.2 us
  transfers between devices with their start and end apart: 12, of which 10 were waited for; matrix products, arithmetic and copies ran while one was open for 9% of the time, Pallas kernels for 0%

commit v1 on v0

--- a/solution.py
+++ b/solution.py
@@ -1,9 +1,13 @@
 from functools import partial
 import math
+
+from types import SimpleNamespace
 
 import jax
 import jax.numpy as jnp
 from jax import lax
+from jax.experimental import pallas as pl
+from jax.experimental.pallas import tpu as pltpu
 from jax.sharding import PartitionSpec as P
 
 D = 768
@@ -13,9 +17,251 @@
 BLOCK = 16
 SEGS = 3
 SEQ_TOK = 64
-
-
 EPSILON = 1e-05
+
+F32 = jnp.float32
+BF16 = jnp.bfloat16
+MESH = pl.DeviceIdType.MESH
+MICRO = 2
+SLOT = 2 * SEQ_TOK
+ROWS = MICRO * SLOT
+PAIRS = HEADS // 2
+LANES = 128
+PART = 48
+UNITS = 12
+WIDE = 768
+SCALE = HEAD_DIM ** (-0.5)
+
+UNIT_LEFT = (0, 1, 2, 3, 4, 4, 4, 4, 5, 6, 6, 6)
+UNIT_RIGHT = (0, 0, 0, 0, 1, 2, 3, 4, 5, 6, 7, 8)
+LEFTS = 7
+RIGHTS = 9
+SUM_Z_FIRST = 2
+
+
+def dot(a, b):
+    return jnp.dot(a, b, preferred_element_type=F32)
+
+
+def dot_nt(a, b):
+    return lax.dot_general(a, b, (((1,), (1,)), ((), ())), preferred_element_type=F32)
+
+
+def dot_tn(a, b):
+    return lax.dot_general(a, b, (((0,), (0,)), ((), ())), preferred_element_type=F32)
+
+
+def normalize(values):
+    centred = values - jnp.mean(values, axis=-1, keepdims=True)
+    inverse = lax.rsqrt(jnp.mean(centred * centred, axis=-1, keepdims=True) + EPSILON)
+    return centred * inverse, inverse
+
+
+def normal_back(d_normed, normed, inverse):
+    return inverse * (
+        d_normed
+        - jnp.mean(d_normed, axis=-1, keepdims=True)
+        - normed * jnp.mean(d_normed * normed, axis=-1, keepdims=True)
+    )
+
+
+def token_tables(token, first, second):
+    one = (token >= first).astype(jnp.int32)
+    two = (token >= first + second).astype(jnp.int32)
+    return one + two, token - one * first - two * second
+
+
+def swap_halves(values):
+    lane = lax.broadcasted_iota(jnp.int32, values.shape, 1)
+    low = (lane % HEAD_DIM) < HEAD_DIM // 2
+    up = pltpu.roll(values, LANES - HEAD_DIM // 2, 1)
+    down = pltpu.roll(values, HEAD_DIM // 2, 1)
+    return jnp.where(low, up, down)
+
+
+def head_masked(pair):
+    lane = lax.broadcasted_iota(jnp.int32, pair.shape, 1)
+    zero = jnp.zeros_like(pair)
+    return jnp.concatenate(
+        [jnp.where(lane < HEAD_DIM, pair, zero), jnp.where(lane < HEAD_DIM, zero, pair)], axis=0
+    )
+
+
+def build_tables(lengths, cos_t, sin_t, mask_t):
+    for m in range(MICRO):
+        first, second = lengths[m, 0], lengths[m, 1]
+        row = lax.broadcasted_iota(jnp.int32, (SLOT, LANES), 0)
+        col = lax.broadcasted_iota(jnp.int32, (SLOT, LANES), 1)
+        doc_r, pos_r = token_tables(row % SEQ_TOK, first, second)
+        doc_c, pos_c = token_tables(col % SEQ_TOK, first, second)
+        block_r, block_c = pos_r // BLOCK, pos_c // BLOCK
+        noisy_r, noisy_c = row < SEQ_TOK, col < SEQ_TOK
+        same = (doc_r == doc_c) & (doc_r < SEGS - 1)
+        ruling = (noisy_r & noisy_c & (block_r == block_c)) | (
+            jnp.logical_not(noisy_c)
+            & (
+                (noisy_r & (block_c < block_r))
+                | (jnp.logical_not(noisy_r) & (block_c <= block_r))
+            )
+        )
+        allowed = (same & ruling) | (row == col)
+        mask_t[m] = jnp.where(allowed, 1.0, 0.0)
+        half = HEAD_DIM // 2
+        frequency = jnp.exp((col % half).astype(F32) * (-2.0 * math.log(10000.0) / HEAD_DIM))
+        angle = pos_r.astype(F32) * frequency
+        sign = jnp.where((col % HEAD_DIM) < half, -1.0, 1.0)
+        cos_t[m] = jnp.cos(angle)
+        sin_t[m] = jnp.sin(angle) * sign
+
+
+def rotate_pair(values, cosine, sine):
+    return values * cosine + swap_halves(values) * sine
+
+
+def gelu_both(v):
+    c = math.sqrt(2.0 / math.pi)
+    square = v * v
+    t = jnp.tanh(c * (v + 0.044715 * (v * square)))
+    half = 0.5 * (1.0 + t)
+    slope = half + (0.5 * c) * v * (1.0 - t * t) * (1.0 + (3.0 * 0.044715) * square)
+    return v * half, slope
+
+
+def forward(R, m, waits):
+    rows = pl.ds(pl.multiple_of(m * SLOT, SLOT), SLOT)
+    lane = lax.broadcasted_iota(jnp.int32, (SLOT, LANES), 1)
+    normed, inverse = normalize(R.x[rows, :].astype(F32))
+    R.normed[rows, :] = normed
+    R.inv[rows, :] = jnp.broadcast_to(inverse, (SLOT, LANES))
+    entry = (normed * R.gain_a[...]).astype(BF16)
+    R.entry[rows, :] = entry
+    waits(0)
+    cosine, sine = R.cos[m], R.sin[m]
+    for t in range(9):
+        joined = dot(entry, R.w_qkv[:, t * 256 : (t + 1) * 256])
+        kept = (R.q, R.k, R.v)[t // 3]
+        for j in range(2):
+            at = (t * 256 + j * LANES) % D
+            piece = joined[:, j * LANES : (j + 1) * LANES]
+            if t < 6:
+                piece = rotate_pair(piece, cosine, sine)
+            kept[rows, at : at + LANES] = piece.astype(BF16)
+    keep = jnp.concatenate([R.mask[m], R.mask[m]], axis=0) > 0.5
+    for p in range(PAIRS):
+        lanes = pl.ds(p * LANES, LANES)
+        q2 = head_masked(R.q[rows, lanes])
+        raw = dot_nt(q2, R.k[rows, lanes]) * SCALE
+        scores = jnp.where(keep, raw, -1e30)
+        exponent = jnp.exp(scores - jnp.max(scores, axis=-1, keepdims=True))
+        probs = exponent / jnp.sum(exponent, axis=-1, keepdims=True)
+        R.probs[m * PAIRS + p] = probs
+        pv = dot(probs.astype(BF16), R.v[rows, lanes])
+        R.mixed[rows, lanes] = jnp.where(lane < HEAD_DIM, pv[:SLOT], pv[SLOT:]).astype(BF16)
+    waits(1)
+    hidden = R.x[rows, :].astype(F32) + dot(R.mixed[rows, :], R.w_out[...])
+    R.hidden[rows, :] = hidden
+    normed, inverse = normalize(hidden)
+    R.normed2[rows, :] = normed
+    R.inv2[rows, :] = jnp.broadcast_to(inverse, (SLOT, LANES))
+    entry2 = (normed * R.gain_b[...]).astype(BF16)
+    R.entry2[rows, :] = entry2
+    waits(2)
+    for t in range(FF // 256):
+        cols = pl.ds(t * 256, 256)
+        inner = dot(entry2, R.w_up[:, cols]) + R.b_up[:, cols]
+        act, slope = gelu_both(inner)
+        R.act[rows, cols] = act.astype(BF16)
+        R.slope[rows, cols] = slope
+    waits(3)
+    R.y[rows, :] = (
+        R.hidden[rows, :] + dot(R.act[rows, :], R.w_down[...]) + R.b_down[...]
+    ).astype(BF16)
+
+
+def backward_feed(R):
+    g = R.right[0]
+    for t in range(12):
+        d_act = dot_nt(g, R.w_down[t * 256 : (t + 1) * 256, :])
+        d_inner = (R.slope[:, t * 256 : (t + 1) * 256] * d_act).astype(BF16)
+        R.right[1 + t // 3, :, (t % 3) * 256 : (t % 3 + 1) * 256] = d_inner
+        R.vec[3 + t // 3 : 4 + t // 3, (t % 3) * 256 : (t % 3 + 1) * 256] = jnp.sum(
+            d_inner.astype(F32), axis=0, keepdims=True
+        )
+    R.vec[2:3, :] = jnp.sum(g.astype(F32), axis=0, keepdims=True)
+    for t in range(3):
+        rows = pl.ds(t * 256, 256)
+        total = dot_nt(R.right[1], R.w_up[rows, 0:WIDE])
+        for j in range(1, 4):
+            total += dot_nt(R.right[1 + j], R.w_up[rows, j * WIDE : (j + 1) * WIDE])
+        R.hidden[:, rows] = total
+    gain = jnp.zeros((1, D), F32)
+    for m in range(MICRO):
+        rows = pl.ds(m * SLOT, SLOT)
+        d_entry = R.hidden[rows, :]
+        normed = R.normed2[rows, :]
+        gain += jnp.sum(d_entry * normed, axis=0, keepdims=True)
+        d_hidden = R.right[0, rows, :].astype(F32) + normal_back(
+            d_entry * R.gain_b[...], normed, R.inv2[rows, 0:1]
+        )
+        R.hidden[rows, :] = d_hidden
+        R.right[5, rows, :] = d_hidden.astype(BF16)
+    R.vec[1:2, :] = gain
+
+
+def backward_attention(R, m):
+    rows = pl.ds(pl.multiple_of(m * SLOT, SLOT), SLOT)
+    R.d_mixed[rows, :] = dot_nt(R.right[5, rows, :], R.w_out[...]).astype(BF16)
+    cosine, sine = R.cos[m], -R.sin[m]
+    for p in range(PAIRS):
+        lanes = pl.ds(p * LANES, LANES)
+        dm2 = head_masked(R.d_mixed[rows, lanes])
+        q2 = head_masked(R.q[rows, lanes])
+        k2 = head_masked(R.k[rows, lanes])
+        probs = R.probs[m * PAIRS + p]
+        d_probs = dot_nt(dm2, R.v[rows, lanes])
+        d_scores = (
+            probs * (d_probs - jnp.sum(probs * d_probs, axis=-1, keepdims=True))
+        ).astype(BF16)
+        d_values = dot_tn(probs.astype(BF16), dm2)
+        side = jnp.concatenate([d_scores[:SLOT], d_scores[SLOT:]], axis=1)
+        d_query = dot(side, k2) * SCALE
+        d_keys = dot_tn(d_scores, q2) * SCALE
+        R.right[6, rows, lanes] = rotate_pair(d_query, cosine, sine).astype(BF16)
+        R.right[7, rows, lanes] = rotate_pair(d_keys, cosine, sine).astype(BF16)
+        R.right[8, rows, lanes] = d_values.astype(BF16)
+    d_entry = jnp.zeros((SLOT, D), F32)
+    for t in range(3):
+        d_entry += dot_nt(R.right[6 + t, rows, :], R.w_qkv[:, t * WIDE : (t + 1) * WIDE])
+    normed = R.normed[rows, :]
+    R.vec[0:1, :] = R.vec[0:1, :] + jnp.sum(d_entry * normed, axis=0, keepdims=True)
+    R.d_state[rows, :] = (
+        R.hidden[rows, :] + normal_back(d_entry * R.gain_a[...], normed, R.inv[rows, 0:1])
+    ).astype(BF16)
+
+
+def turn_lefts(R, core):
+    def place(kind, owner_core, chip, block):
+        x, z = chip % 2, chip // 2
+
+        @pl.when(core == owner_core)
+        def _():
+            R.left[kind, x * 4 + z] = block
+
+        @pl.when(core != owner_core)
+        def _():
+            R.left_out[kind, x * 4 + z] = block
+
+    for kind, factor in ((4, R.entry2), (5, R.mixed), (6, R.entry)):
+        turned = factor[...].T
+        for d in range(16):
+            place(kind, d % 2, d // 2, turned[d * PART : (d + 1) * PART, :])
+    for d4 in range(4):
+        turned = R.act[:, d4 * 768 : (d4 + 1) * 768].T
+        for e in range(4):
+            d = d4 * 4 + e
+            for i in range(4):
+                at = e * 192 + i * PART
+                place(i, d % 2, d // 2, turned[at : at + PART, :])
 
 
 def passed_along(block, axis, distance):
@@ -90,13 +336,13 @@
     )
 
 
-def normalize(values):
+def plain_normalize(values):
     centred = values - jnp.mean(values, axis=-1, keepdims=True)
     inverse = lax.rsqrt(jnp.mean(centred * centred, axis=-1, keepdims=True) + EPSILON)
     return (centred * inverse, inverse)
 
 
-def normal_back(d_normed, normed, inverse):
+def plain_normal_back(d_normed, normed, inverse):
     return inverse * (
         d_normed
         - jnp.mean(d_normed, axis=-1, keepdims=True)
@@ -116,7 +362,7 @@
     allowed, cosine, sine = row_tables(lengths_row)
     count = state.shape[0]
     widened = state.astype(jnp.float32)
-    normed, inverse = normalize(widened)
+    normed, inverse = plain_normalize(widened)
     entry = (normed * gain_a).astype(jnp.bfloat16)
     joined = jnp.dot(entry, w_qkv, preferred_element_type=jnp.float32)
     query = rotate(joined[:, :D].reshape(count, HEADS, HEAD_DIM), cosine, sine).astype(jnp.bfloat16)
@@ -136,7 +382,7 @@
         .astype(jnp.bfloat16)
     )
     hidden = widened + jnp.dot(mixed, w_out, preferred_element_type=jnp.float32)
-    normed_two, inverse_two = normalize(hidden)
+    normed_two, inverse_two = plain_normalize(hidden)
     entry_two = (normed_two * gain_b).astype(jnp.bfloat16)
     inner = jnp.dot(entry_two, w_up, preferred_element_type=jnp.float32) + b_up
     activated = jax.nn.gelu(inner, approximate=True).astype(jnp.bfloat16)
@@ -219,7 +465,7 @@
     d_entry_two = jnp.einsum("rf,df->rd", d_inner, w_up, preferred_element_type=jnp.float32)
     grad_gain_b = jnp.sum(d_entry_two * normed_two, axis=0)
     feed_group = settle(0, (grad_gain_b, grad_up, grad_bias_up, grad_down, grad_bias_down))
-    d_hidden = upper + normal_back(d_entry_two * gain_b, normed_two, inverse_two)
+    d_hidden = upper + plain_normal_back(d_entry_two * gain_b, normed_two, inverse_two)
     d_branch = d_hidden.astype(jnp.bfloat16)
     grad_out = jnp.einsum("rd,re->de", mixed, d_branch, preferred_element_type=jnp.float32)
     d_mixed = (
@@ -255,7 +501,7 @@
     d_entry = jnp.einsum("re,de->rd", d_joined, w_qkv, preferred_element_type=jnp.float32)
     grad_gain_a = jnp.sum(d_entry * normed, axis=0)
     attn_group = settle(1, (grad_gain_a, grad_qkv, grad_out))
-    d_state = (d_hidden + normal_back(d_entry * gain_a, normed, inverse)).astype(jnp.bfloat16)
+    d_state = (d_hidden + plain_normal_back(d_entry * gain_a, normed, inverse)).astype(jnp.bfloat16)
     return (d_state, tuple(attn_group) + tuple(feed_group))
 
 
@@ -298,7 +544,7 @@
     )
 
 
-def on_device(
+def plain_device(
     inputs, cotangent, lengths, gain_one, w_qkv, w_out, gain_two, w_up, b_up, w_down, b_down
 ):
     section = lax.axis_index("section")
@@ -361,6 +607,511 @@
     )
 
 
+VMEM = pl.BlockSpec(memory_space=pltpu.VMEM)
+SMEM = pl.BlockSpec(memory_space=pltpu.SMEM)
+ANY = pl.BlockSpec(memory_space=pl.ANY)
+IN = dict(
+    inputs=ANY, cotangent=ANY, lengths=SMEM, gain_a=VMEM, w_qkv_in=ANY, w_out_in=ANY,
+    gain_b=VMEM, w_up_in=ANY, b_up=VMEM, w_down_in=ANY, b_down=VMEM,
+)
+OUT = dict(
+    y=((ROWS, D), BF16),
+    d_state=((ROWS, D), BF16),
+    sum_qkv=((PART, 3 * D), F32),
+    sum_out=((PART, D), F32),
+    sum_up=((PART, FF), F32),
+    sum_down=((4 * PART, D), F32),
+    vec_sum=((8, WIDE), F32),
+)
+EVERY, INNER, OUTER = range(3)
+DEPTH = 2
+A_UNITS = UNITS - SUM_Z_FIRST
+
+SCRATCH = dict(
+    w_qkv=((D, 3 * D), BF16),
+    w_out=((D, D), BF16),
+    w_up=((D, FF), BF16),
+    w_down=((FF, D), BF16),
+    x=((ROWS, D), BF16),
+    cos=((MICRO, SLOT, LANES), F32),
+    sin=((MICRO, SLOT, LANES), F32),
+    mask=((MICRO, SLOT, SLOT), F32),
+    normed=((ROWS, D), F32),
+    inv=((ROWS, LANES), F32),
+    entry=((ROWS, D), BF16),
+    q=((ROWS, D), BF16),
+    k=((ROWS, D), BF16),
+    v=((ROWS, D), BF16),
+    probs=((MICRO * PAIRS, 2 * SLOT, SLOT), F32),
+    mixed=((ROWS, D), BF16),
+    hidden=((ROWS, D), F32),
+    normed2=((ROWS, D), F32),
+    inv2=((ROWS, LANES), F32),
+    entry2=((ROWS, D), BF16),
+    act=((ROWS, FF), BF16),
+    slope=((ROWS, FF), F32),
+    d_mixed=((ROWS, D), BF16),
+    d_entry=((ROWS, D), F32),
+    right=((RIGHTS, ROWS, WIDE), BF16),
+    right_in=((RIGHTS, ROWS, WIDE), BF16),
+    left=((LEFTS, 8, PART, ROWS), BF16),
+    left_out=((LEFTS, 8, PART, ROWS), BF16),
+    left_in=((LEFTS, 8, PART, ROWS), BF16),
+    grad=((UNITS, 2, 4, PART, WIDE), BF16),
+    ax=((A_UNITS, 4, PART, WIDE), BF16),
+    az=((A_UNITS, 5, PART, WIDE), BF16),
+    bz=((SUM_Z_FIRST, 5, 2, PART, WIDE), BF16),
+    bs=((SUM_Z_FIRST, PART, WIDE), BF16),
+    bx=((SUM_Z_FIRST, PART, WIDE), BF16),
+    vec=((8, WIDE), F32),
+    vec_in=((5, 8, WIDE), F32),
+    vec_part=((3, 8, WIDE), F32),
+)
+SEMS = dict(
+    load=(5,), ys=(4,), yr=(4,), ls=(4,), lr=(4,), rs=(4,), rr=(4,),
+    axs=(A_UNITS,), axr=(A_UNITS,), azs=(A_UNITS, 5), azr=(A_UNITS, 5),
+    bzs=(SUM_Z_FIRST, 5), bzr=(SUM_Z_FIRST, 5), bxs=(SUM_Z_FIRST,), bxr=(SUM_Z_FIRST,),
+    vs=(5,), vr=(5,),
+)
+LEFT_GROUPS = ((0, 4), (4, 1), (5, 1), (6, 1))
+RIGHT_GROUPS = ((0, 1), (1, 4), (5, 1), (6, 3))
+
+
+def kernel(*refs):
+    names = (*IN, *OUT, *SCRATCH, *SEMS)
+    R = SimpleNamespace(**dict(zip(names, refs)))
+    place, section = lax.axis_index("dp"), lax.axis_index("section")
+    core, x, z = place % 2, (place // 2) % 2, place // 4
+    half = z // 2
+    outer = (z == 0) | (z == 3)
+    inner = (z == 1) | (z == 2)
+
+    def dp_of(z_, x_, core_):
+        return (z_ * 4 + x_ * 2 + core_, section)
+
+    near_core = dp_of(z, x, 1 - core)
+    near_x = dp_of(z, 1 - x, core)
+    near_y = (place, 1 - section)
+    near_side = dp_of(half * 2 + 1 - z % 2, x, core)
+    near_mid = dp_of(3 - z, x, core)
+
+    owners = [j + half * (3 - 2 * j) for j in range(4)]
+
+    def owner(j):
+        return owners[j]
+
+    def copy(src, dst, send, recv, device):
+        return pltpu.make_async_remote_copy(
+            src_ref=src, dst_ref=dst, send_sem=send, recv_sem=recv,
+            device_id=device, device_id_type=MESH,
+        )
+
+    weights_in = (R.w_qkv_in, R.w_out_in, R.w_up_in, R.w_down_in)
+    weights = (R.w_qkv, R.w_out, R.w_up, R.w_down)
+    loads = [
+        pltpu.make_async_copy(src, dst, R.load.at[i])
+        for i, (src, dst) in enumerate(zip(weights_in, weights))
+    ]
+    for load in loads:
+        load.start()
+
+    def take(index, src, dst):
+        @pl.when(section == index)
+        def _():
+            pltpu.make_async_copy(src, dst, R.load.at[4]).start()
+
+    def taken(index, src, dst):
+        @pl.when(section == index)
+        def _():
+            pltpu.make_async_copy(src, dst, R.load.at[4]).wait()
+
+    take(0, R.inputs, R.x)
+    take(1, R.cotangent, R.right.at[0])
+
+    barrier = pltpu.get_barrier_semaphore()
+    for device in (near_core, near_x, near_y, near_side):
+        pl.semaphore_signal(barrier, inc=1, device_id=device, device_id_type=MESH)
+
+    @pl.when(inner)
+    def _():
+        pl.semaphore_signal(barrier, inc=1, device_id=near_mid, device_id_type=MESH)
+
+    build_tables(R.lengths, R.cos, R.sin, R.mask)
+
+    @pl.when(inner)
+    def _():
+        pl.semaphore_wait(barrier, 5)
+
+    @pl.when(outer)
+    def _():
+        pl.semaphore_wait(barrier, 4)
+
+    def x_copy(m):
+        rows = pl.ds(m * SLOT, SLOT)
+        return copy(R.y.at[rows], R.x.at[rows], R.ys.at[m], R.yr.at[m], near_y)
+
+    def g_copy(m):
+        rows = pl.ds(m * SLOT, SLOT)
+        return copy(
+            R.d_state.at[rows], R.right.at[0, rows], R.ys.at[2 + m], R.yr.at[2 + m], near_y
+        )
+
+    taken(0, R.inputs, R.x)
+    for m in range(MICRO):
+
+        @pl.when(section == 1)
+        def _():
+            x_copy(m).wait_recv()
+
+        forward(R, m, lambda n: loads[n].wait() if m == 0 else None)
+
+        @pl.when(section == 0)
+        def _():
+            x_copy(m).start()
+
+    def left_copy(i):
+        a, n = LEFT_GROUPS[i]
+        rows = pl.ds(a, n)
+        return copy(
+            R.left_out.at[rows], R.left_in.at[rows], R.ls.at[i], R.lr.at[i], near_core
+        )
+
+    def right_copy(i):
+        a, n = RIGHT_GROUPS[i]
+        rows = pl.ds(a, n)
+        return copy(
+            R.right.at[rows], R.right_in.at[rows], R.rs.at[i], R.rr.at[i], near_core
+        )
+
+    def send_lefts():
+        turn_lefts(R, core)
+        for i in range(4):
+            left_copy(i).start()
+
+    @pl.when(section == 0)
+    def _():
+        send_lefts()
+        for m in range(MICRO):
+            g_copy(m).wait_recv()
+
+    taken(1, R.cotangent, R.right.at[0])
+
+    def weight_unit(u):
+        left, right = UNIT_LEFT[u], UNIT_RIGHT[u]
+        own = R.left[left].reshape(8 * PART, ROWS)
+        other = R.left_in[left].reshape(8 * PART, ROWS)
+        total = dot(own, R.right[right]) + dot(other, R.right_in[right])
+        R.grad[u] = total.astype(BF16).reshape(2, 4, PART, WIDE)
+
+    def finish(u, total):
+        if u < 4:
+            R.sum_down[u * PART : (u + 1) * PART, :] = total
+        elif u < 8:
+            R.sum_up[:, (u - 4) * WIDE : (u - 3) * WIDE] = total
+        elif u == 8:
+            R.sum_out[...] = total
+        else:
+            R.sum_qkv[:, (u - 9) * WIDE : (u - 8) * WIDE] = total
+
+    started = {}
+
+    def start(condition, make, *operands):
+        started[(condition, make) + operands[:1] + operands[-2:-1]] = (condition, make, operands)
+        make(*operands).start()
+
+    def ax_copy(i):
+        u = i + SUM_Z_FIRST
+        return copy(R.grad.at[u, 1 - x], R.ax.at[i], R.axs.at[i], R.axr.at[i], near_x)
+
+    def az_copy(i, src, at, slot, device):
+        return copy(
+            src.at[at], R.az.at[i, slot], R.azs.at[i, slot], R.azr.at[i, slot], device
+        )
+
+    def a0(i):
+        start(EVERY, ax_copy, i)
+
+    def a1(i):
+        ax_copy(i).wait_recv()
+        for j in range(4):
+            R.ax[i, j] = R.ax[i, j] + R.grad[i + SUM_Z_FIRST, x, j]
+
+        @pl.when(outer)
+        def _():
+            for j in (3, 2, 1):
+                start(OUTER, az_copy, i, R.ax, (i, owner(j)), j - 1, near_side)
+
+    def a2(i):
+        @pl.when(inner)
+        def _():
+            for j in (3, 2):
+                az_copy(i, R.az, (i, j - 1), j - 1, near_side).wait_recv()
+                R.az[i, j - 1] = R.az[i, j - 1] + R.ax[i, owner(j)]
+                start(INNER, az_copy, i, R.az, (i, j - 1), 6 - j, near_mid)
+
+    def a3(i):
+        @pl.when(inner)
+        def _():
+            az_copy(i, R.az, (i, 3), 3, near_mid).wait_recv()
+            R.az[i, 3] = R.az[i, 3] + R.ax[i, owner(0)]
+            start(INNER, az_copy, i, R.az, (i, 3), 0, near_side)
+
+    def a4(i):
+        u = i + SUM_Z_FIRST
+
+        @pl.when(inner)
+        def _():
+            az_copy(i, R.az, (i, 0), 0, near_side).wait_recv()
+            az_copy(i, R.az, (i, 4), 4, near_mid).wait_recv()
+            finish(
+                u,
+                R.ax[i, owner(1)].astype(F32)
+                + R.az[i, 0].astype(F32)
+                + R.az[i, 4].astype(F32),
+            )
+
+        @pl.when(outer)
+        def _():
+            az_copy(i, R.az, (i, 0), 0, near_side).wait_recv()
+            finish(u, R.ax[i, owner(0)].astype(F32) + R.az[i, 0].astype(F32))
+
+    def bz_copy(i, src, at, slot, device):
+        return copy(
+            src.at[at], R.bz.at[i, slot], R.bzs.at[i, slot], R.bzr.at[i, slot], device
+        )
+
+    def bx_copy(i):
+        return copy(R.bs.at[i], R.bx.at[i], R.bxs.at[i], R.bxr.at[i], near_x)
+
+    def b0(i):
+        @pl.when(outer)
+        def _():
+            for j in (3, 2, 1):
+                start(OUTER, bz_copy, i, R.grad, (i, slice(None), owner(j)), j - 1, near_side)
+
+    def b1(i):
+        @pl.when(inner)
+        def _():
+            for j in (3, 2):
+                bz_copy(i, R.bz, (i, j - 1), j - 1, near_side).wait_recv()
+                for a in range(2):
+                    R.bz[i, j - 1, a] = R.bz[i, j - 1, a] + R.grad[i, a, owner(j)]
+                start(INNER, bz_copy, i, R.bz, (i, j - 1), 6 - j, near_mid)
+
+    def b2(i):
+        @pl.when(inner)
+        def _():
+            bz_copy(i, R.bz, (i, 3), 3, near_mid).wait_recv()
+            for a in range(2):
+                R.bz[i, 3, a] = R.bz[i, 3, a] + R.grad[i, a, owner(0)]
+            start(INNER, bz_copy, i, R.bz, (i, 3), 0, near_side)
+
+    def b_total(i, a):
+        own = R.grad[i, a, z].astype(F32) + R.bz[i, 0, a].astype(F32)
+        return own
+
+    def b3(i):
+        @pl.when(inner)
+        def _():
+            bz_copy(i, R.bz, (i, 0), 0, near_side).wait_recv()
+            bz_copy(i, R.bz, (i, 4), 4, near_mid).wait_recv()
+            R.bs[i] = (b_total(i, 1 - x) + R.bz[i, 4, 1 - x].astype(F32)).astype(BF16)
+
+        @pl.when(outer)
+        def _():
+            bz_copy(i, R.bz, (i, 0), 0, near_side).wait_recv()
+            R.bs[i] = b_total(i, 1 - x).astype(BF16)
+
+        start(EVERY, bx_copy, i)
+
+    def b4(i):
+        bx_copy(i).wait_recv()
+
+        @pl.when(inner)
+        def _():
+            finish(i, b_total(i, x) + R.bz[i, 4, x].astype(F32) + R.bx[i].astype(F32))
+
+        @pl.when(outer)
+        def _():
+            finish(i, b_total(i, x) + R.bx[i].astype(F32))
+
+    def v_copy(stage, src, at, device):
+        return copy(src.at[at] if at is not None else src, R.vec_in.at[stage], R.vs.at[stage], R.vr.at[stage], device)
+
+    def v0():
+        start(EVERY, v_copy, 0, R.vec, None, near_core)
+
+    def v1():
+        v_copy(0, R.vec, None, near_core).wait_recv()
+        R.vec_part[0] = R.vec[...] + R.vec_in[0]
+        start(EVERY, v_copy, 1, R.vec_part, 0, near_x)
+
+    def v2():
+        v_copy(1, R.vec_part, 0, near_x).wait_recv()
+        R.vec_part[1] = R.vec_part[0] + R.vec_in[1]
+
+        @pl.when(outer)
+        def _():
+            start(OUTER, v_copy, 2, R.vec_part, 1, near_side)
+
+    def v3():
+        @pl.when(inner)
+        def _():
+            v_copy(2, R.vec_part, 1, near_side).wait_recv()
+            R.vec_part[2] = R.vec_part[1] + R.vec_in[2]
+            start(INNER, v_copy, 3, R.vec_part, 2, near_mid)
+
+    def v4():
+        @pl.when(inner)
+        def _():
+            v_copy(3, R.vec_part, 2, near_mid).wait_recv()
+            R.vec_sum[...] = R.vec_part[2] + R.vec_in[3]
+            start(INNER, v_copy, 4, R.vec_sum, None, near_side)
+
+    def v5():
+        @pl.when(outer)
+        def _():
+            v_copy(4, R.vec_part, 2, near_side).wait_recv()
+            R.vec_sum[...] = R.vec_in[4]
+
+    def first_units():
+        left_copy(0).wait_recv()
+        right_copy(0).wait_recv()
+        for u, send, i in ((0, b0, 0), (2, a0, 0), (1, b0, 1), (3, a0, 1)):
+            weight_unit(u)
+            send(i)
+
+    right_copy(0).start()
+    R.vec[...] = jnp.zeros((8, WIDE), F32)
+    pl.when(section == 0)(first_units)
+    backward_feed(R)
+    right_copy(1).start()
+    right_copy(2).start()
+    for m in range(MICRO):
+        backward_attention(R, m)
+
+        @pl.when(section == 1)
+        def _():
+            g_copy(m).start()
+
+    right_copy(3).start()
+
+    @pl.when(section == 1)
+    def _():
+        send_lefts()
+        first_units()
+
+    for i in range(1, 4):
+        left_copy(i).wait_recv()
+        right_copy(i).wait_recv()
+
+    events = []
+    for u in range(4, UNITS):
+        i = u - SUM_Z_FIRST
+        events += [(0.0, weight_unit, u)]
+        if i < DEPTH:
+            events += [(0.0, a0, i)]
+    for i, t in enumerate((7.0, 16.0)):
+        events += [(t, b1, i), (t + 4, b2, i), (t + 8, b3, i), (t + 12, b4, i)]
+    for i in range(A_UNITS):
+        t1 = 6.4 * (i + 1)
+        t2 = max(t1 + 6.0, 20.0 + 4.7 * (i + 1))
+        events += [(t1, a1, i), (t2, a2, i), (t2 + 3.5, a3, i), (t2 + 7.0, a4, i)]
+        if i + DEPTH < A_UNITS:
+            events += [(t1, a0, i + DEPTH)]
+    for i, step in enumerate((v0, v1, v2, v3, v4, v5)):
+        events += [(20.0 + 4.0 * i, step, None)]
+    for _, step, index in sorted(events, key=lambda e: e[0]):
+        step() if index is None else step(index)
+
+    for i in range(4):
+        left_copy(i).wait_send()
+        right_copy(i).wait_send()
+
+    def wait_sent(name):
+        for condition, make, operands in started.values():
+            if condition == name:
+                make(*operands).wait_send()
+
+    wait_sent(EVERY)
+    pl.when(inner)(lambda: wait_sent(INNER))
+    pl.when(outer)(lambda: wait_sent(OUTER))
+
+    for m in range(MICRO):
+
+        @pl.when(section == 0)
+        def _():
+            x_copy(m).wait_send()
+
+        @pl.when(section == 1)
+        def _():
+            g_copy(m).wait_send()
+
+
+def settle(vec, *refs):
+    arrays, narrow, wide, sems = refs[:6], refs[6:10], refs[10:16], refs[16]
+    copies = [pltpu.make_async_copy(a, w, sems.at[i]) for i, (a, w) in enumerate(zip(arrays, wide))]
+    for item in copies:
+        item.start()
+    place = lax.axis_index("dp")
+    near = pltpu.roll(vec[...], (16 - place) % 16 * PART, 1)
+    for i in range(3):
+        narrow[i][...] = near[i : i + 1, :PART]
+    far = pltpu.roll(vec[...], (4 - place % 4) % 4 * (4 * PART), 1)
+    row = lax.broadcasted_iota(jnp.int32, far.shape, 0)
+    mine = jnp.sum(jnp.where(row == 3 + place // 4, far, 0.0), axis=0, keepdims=True)
+    narrow[3][...] = mine[:, : 4 * PART]
+    for item in copies:
+        item.wait()
+
+
+def layer_device(
+    inputs, cotangent, lengths, gain_one, w_qkv, w_out, gain_two, w_up, b_up, w_down, b_down
+):
+    y, d_state, qkv, out, up, down, vec = pl.pallas_call(
+        kernel,
+        out_shape=[jax.ShapeDtypeStruct(s, d) for s, d in OUT.values()],
+        in_specs=list(IN.values()),
+        out_specs=[VMEM] * len(OUT),
+        scratch_shapes=[pltpu.VMEM(s, d) for s, d in SCRATCH.values()]
+        + [pltpu.SemaphoreType.DMA(s) for s in SEMS.values()],
+        compiler_params=pltpu.CompilerParams(
+            collective_id=0, has_side_effects=True, vmem_limit_bytes=60 * 2**20
+        ),
+        name="layers",
+    )(
+        inputs.reshape(ROWS, D), cotangent.reshape(ROWS, D), lengths[:, 0], gain_one, w_qkv[0],
+        w_out[0], gain_two, w_up[0], b_up, w_down[0], b_down,
+    )
+    totals = pl.pallas_call(
+        settle,
+        out_shape=[
+            jax.ShapeDtypeStruct((1, PART), F32),
+            jax.ShapeDtypeStruct((1, PART), F32),
+            jax.ShapeDtypeStruct((1, PART), F32),
+            jax.ShapeDtypeStruct((1, 4 * PART), F32),
+        ]
+        + [jax.ShapeDtypeStruct(s, d) for s, d in list(OUT.values())[:6]],
+        in_specs=[VMEM] * 7,
+        out_specs=[VMEM] * 4 + [ANY] * 6,
+        scratch_shapes=[pltpu.SemaphoreType.DMA((6,))],
+        name="settle",
+    )(vec, y, d_state, qkv, out, up, down)
+    gain_a, gain_b, bias_down, bias_up, y, d_state, qkv, out, up, down = totals
+    return (
+        y.reshape(1, MICRO, SLOT, D),
+        d_state.reshape(1, MICRO, SLOT, D),
+        gain_a,
+        qkv[None],
+        out[None],
+        gain_b,
+        up[None],
+        bias_up,
+        down[None],
+        bias_down,
+    )
+
+
 def solution(mesh):
     placed = (
         P(None, "dp", None),
@@ -376,7 +1127,7 @@
         P("section", None),
     )
     return jax.shard_map(
-        on_device,
+        layer_device if mesh.shape["dp"] == 16 else plain_device,
         mesh=mesh,
         in_specs=placed,
         out_specs=(

time: 989 us -> 142 us (0.14)
  waiting for transfers between devices: 644 us -> 0 us
  Pallas kernels: 0 us -> 140 us
  other arithmetic: 123 us -> 0 us
  matrix products: 94.5 us -> 0 us
  local copies, waits for them, and re-layouts: 88.7 us -> 0 us
  between operations: 15.7 us -> 0.84 us
  starting transfers between devices: 14 us -> 0 us
    reduce_scatter x4 -> x0, waiting for transfers between devices: 391 us -> none  [the longest x1 116 us: reduce_total(): lax.psum_scatter(grad_down[None], 'dp', scatter_dimension=1, tiled=True)]
    unnamed x12 -> x0, waiting for transfers between devices: 175 us -> none
    pallas_call x0 -> x2, Pallas kernels: none -> 140 us  [the longest x1 137 us: layer_device(): pl.pallas_call(kernel, out_shape=[jax.ShapeDtypeStruct(s, d) for s, d in...]
    dot_general x38 -> x0, matrix products: 94.5 us -> none  [the longest x2 12.7 us: backward_core(): jnp.einsum('rd,fd->rf', incoming, w_down, preferred_element_type=jnp.floa...]
    ppermute x4 -> x0, waiting for transfers between devices: 77.4 us -> none  [passed_along(): return lax.ppermute(block, axis, route)]
    broadcast_in_dim x4 -> x0, other arithmetic: 44.5 us -> none  [the longest x1 14.8 us: reduce_total(): grad_up[None]]
    dynamic_update_slice x41 -> x0, other arithmetic: 24.7 us -> none  [keep_at(): lax.dynamic_update_index_in_dim(stack, jnp.where(active, leaf, current),...]
    unnamed x194 -> x0, local copies, waits for them, and re-layouts: 20.2 us -> none
  transfers between devices with their start and end apart: 12 -> 0, of which waited for: 10 -> 0; matrix products, arithmetic and copies ran while one was open for 9% -> 0% of each run, Pallas kernels for 0% -> 0%
where the time goes in v1:
time: 142 us; the launch traced here: 141 us
  Pallas kernels  140 us (99%)
    pallas_call x1, Pallas kernels, layer_device(): pl.pallas_call(kernel, out_shape=[jax.ShapeDtypeStruct(s, d) for s, d in...  137 us
    pallas_call x1, Pallas kernels, layer_device(): pl.pallas_call(settle, out_shape=[jax.ShapeDtypeStruct((1, PART), F32), j...  3.78 us

profile of v1, /device:TPU:0, one launch (start us, length us, event | category | flops | bytes accessed | tf_op | source)
XLA Modules:
  0.0 141.3 jit_solution(13742343869393356886)
XLA Ops:
  0.6 136.7 %layers.1 = (bf16[256,768]{1,0:T(8,128)(2,1)}, bf16[256,768]{1,0:T(8,128)(2,1)}, f32[48,2304]{1,0:T(8,128)}, f32[48,768]{1,0:T(8,128)}, f32[48,3072]{1,0:T(8,128...) custom-call(bf16[256,768]{1,0:T(8,128)(2,1)} %bitcast.17, bf16[256,768]{1,0:T(8,128)(2,1)} %bitcast.18, s32[2,3]{1,0:T(2,128)} %bitcast.19, ...), custom_call_target="tpu_custom_call" | custom-call | tf_op jit(solution)/shard_map/layers/pallas_call | solution.py:1071
  137.4 3.8 %settle.1 = (f32[1,48]{1,0:T(1,128)}, f32[1,48]{1,0:T(1,128)}, f32[1,48]{1,0:T(1,128)}, f32[1,192]{1,0:T(1,128)}, bf16[256,768]{1,0:T(8,128)(2,1)}, /*index=5*/b...) custom-call(f32[8,768]{1,0:T(8,128)} %get-tuple-element.27.vec, ...), custom_call_target="tpu_custom_call" | custom-call | tf_op jit(solution)/shard_map/settle/pallas_call | solution.py:1086

commit v2 on v1

--- a/solution.py
+++ b/solution.py
@@ -36,7 +36,6 @@
 UNIT_RIGHT = (0, 0, 0, 0, 1, 2, 3, 4, 5, 6, 7, 8)
 LEFTS = 7
 RIGHTS = 9
-SUM_Z_FIRST = 2
 
 
 def dot(a, b):
@@ -171,29 +170,39 @@
         inner = dot(entry2, R.w_up[:, cols]) + R.b_up[:, cols]
         act, slope = gelu_both(inner)
         R.act[rows, cols] = act.astype(BF16)
-        R.slope[rows, cols] = slope
+        R.slope[rows, cols] = slope * R.slope[rows, cols]
     waits(3)
     R.y[rows, :] = (
         R.hidden[rows, :] + dot(R.act[rows, :], R.w_down[...]) + R.b_down[...]
     ).astype(BF16)
 
 
-def backward_feed(R):
+def feed_inner_matmul(R, t):
     g = R.right[0]
-    for t in range(12):
-        d_act = dot_nt(g, R.w_down[t * 256 : (t + 1) * 256, :])
-        d_inner = (R.slope[:, t * 256 : (t + 1) * 256] * d_act).astype(BF16)
-        R.right[1 + t // 3, :, (t % 3) * 256 : (t % 3 + 1) * 256] = d_inner
-        R.vec[3 + t // 3 : 4 + t // 3, (t % 3) * 256 : (t % 3 + 1) * 256] = jnp.sum(
+    for j in range(3):
+        cols = pl.ds(t * WIDE + j * 256, 256)
+        R.slope[:, cols] = R.slope[:, cols] * dot_nt(g, R.w_down[cols, :])
+
+
+def feed_inner(R, t):
+    for j in range(3):
+        d_inner = R.slope[:, t * WIDE + j * 256 : t * WIDE + (j + 1) * 256].astype(BF16)
+        R.right[1 + t, :, j * 256 : (j + 1) * 256] = d_inner
+        R.vec[3 + t : 4 + t, j * 256 : (j + 1) * 256] = jnp.sum(
             d_inner.astype(F32), axis=0, keepdims=True
         )
-    R.vec[2:3, :] = jnp.sum(g.astype(F32), axis=0, keepdims=True)
-    for t in range(3):
-        rows = pl.ds(t * 256, 256)
-        total = dot_nt(R.right[1], R.w_up[rows, 0:WIDE])
-        for j in range(1, 4):
-            total += dot_nt(R.right[1 + j], R.w_up[rows, j * WIDE : (j + 1) * WIDE])
-        R.hidden[:, rows] = total
+
+
+def feed_entry(R, t):
+    rows = pl.ds(t * 256, 256)
+    total = dot_nt(R.right[1], R.w_up[rows, 0:WIDE])
+    for j in range(1, 4):
+        total += dot_nt(R.right[1 + j], R.w_up[rows, j * WIDE : (j + 1) * WIDE])
+    R.hidden[:, rows] = total
+
+
+def feed_norm(R):
+    R.vec[2:3, :] = jnp.sum(R.right[0].astype(F32), axis=0, keepdims=True)
     gain = jnp.zeros((1, D), F32)
     for m in range(MICRO):
         rows = pl.ds(m * SLOT, SLOT)
@@ -208,11 +217,14 @@
     R.vec[1:2, :] = gain
 
 
-def backward_attention(R, m):
-    rows = pl.ds(pl.multiple_of(m * SLOT, SLOT), SLOT)
-    R.d_mixed[rows, :] = dot_nt(R.right[5, rows, :], R.w_out[...]).astype(BF16)
+def attention_mixed(R):
+    R.d_mixed[...] = dot_nt(R.right[5], R.w_out[...]).astype(BF16)
+
+
+def attention_pairs(R, m, t):
+    rows = pl.ds(m * SLOT, SLOT)
     cosine, sine = R.cos[m], -R.sin[m]
-    for p in range(PAIRS):
+    for p in (2 * t, 2 * t + 1):
         lanes = pl.ds(p * LANES, LANES)
         dm2 = head_masked(R.d_mixed[rows, lanes])
         q2 = head_masked(R.q[rows, lanes])
@@ -229,6 +241,10 @@
         R.right[6, rows, lanes] = rotate_pair(d_query, cosine, sine).astype(BF16)
         R.right[7, rows, lanes] = rotate_pair(d_keys, cosine, sine).astype(BF16)
         R.right[8, rows, lanes] = d_values.astype(BF16)
+
+
+def attention_entry(R, m):
+    rows = pl.ds(m * SLOT, SLOT)
     d_entry = jnp.zeros((SLOT, D), F32)
     for t in range(3):
         d_entry += dot_nt(R.right[6 + t, rows, :], R.w_qkv[:, t * WIDE : (t + 1) * WIDE])
@@ -623,9 +639,109 @@
     sum_down=((4 * PART, D), F32),
     vec_sum=((8, WIDE), F32),
 )
-EVERY, INNER, OUTER = range(3)
-DEPTH = 2
-A_UNITS = UNITS - SUM_Z_FIRST
+SHARED = 4
+Z_UNITS = UNITS - 1
+X_UNITS = UNITS - SHARED
+ORDER = (
+  (
+    (
+        (),
+        (303, 302, 301,),
+        (),
+        (),
+        (),
+        (),
+        (),
+        (),
+        (),
+        (),
+        (19, 18, 17, 16,),
+        (23, 22, 21, 20,),
+        (27, 26, 25, 24,),
+        (),
+        (),
+        (),
+        (),
+        (),
+        (),
+        (107, 106, 105,),
+        (111, 110, 109,),
+        (115, 114, 113,),
+        (),
+        (),
+        (),
+        (600,),
+        (),
+        (),
+        (),
+        (601, 119, 602, 31, 118, 30, 117, 29, 28, 123, 122, 121, 35, 127, 126, 125, 34, 33, 32, 39, 38, 37, 36, 400, 204, 605, 131, 43, 208, 130, 42, 212, 129, 41, 40, 135, 47, 134, 133, 139, 138, 137, 46, 45, 44, 216, 500, 143, 142, 141, 147, 146, 145, 220, 224, 228, 232, 236, 240, 244,),
+    ),
+    (
+        (),
+        (),
+        (),
+        (),
+        (),
+        (),
+        (),
+        (),
+        (),
+        (),
+        (19, 18, 16, 17,),
+        (23, 22, 20, 21,),
+        (27, 26, 24, 25,),
+        (),
+        (),
+        (),
+        (),
+        (),
+        (),
+        (),
+        (),
+        (),
+        (),
+        (),
+        (),
+        (600,),
+        (),
+        (),
+        (),
+        (303, 601, 302, 602, 31, 30, 28, 29, 107, 35, 34, 603, 32, 33, 106, 39, 38, 36, 37, 300, 400, 111, 604, 110, 104, 205, 115, 114, 108, 209, 112, 213, 43, 42, 119, 118, 40, 123, 122, 127, 126, 41, 131, 47, 46, 116, 44, 130, 45, 500, 217, 135, 120, 221, 124, 225, 128, 229, 132, 134, 139, 138, 143, 233, 142, 136, 237, 140, 147, 146, 241, 144, 245,),
+    ),
+  ),
+  (
+    (
+        (),
+        (600, 303, 302, 301,),
+        (19, 18, 17, 16,),
+        (),
+        (),
+        (),
+        (601,),
+        (),
+        (),
+        (),
+        (107, 106, 105,),
+        (602, 111, 110, 109,),
+        (115, 114, 113, 23, 119, 22, 21, 20, 118, 117, 605, 27, 123, 26, 25, 24, 122, 121, 400, 31, 127, 30, 126, 29, 28, 125, 500, 204, 35, 131, 34, 130, 33, 32, 129, 39, 135, 208, 212, 216, 220, 38, 134, 37, 36, 133, 43, 139, 224, 228, 42, 138, 232, 41, 40, 137, 47, 143, 46, 142, 236, 45, 141, 44, 147, 146, 145, 240, 244,),
+    ),
+    (
+        (),
+        (600,),
+        (19, 18, 16, 17,),
+        (),
+        (),
+        (),
+        (),
+        (601,),
+        (),
+        (),
+        (),
+        (),
+        (602, 603, 604, 23, 22, 20, 21, 303, 302, 107, 106, 27, 26, 24, 25, 300, 111, 110, 115, 114, 400, 119, 118, 123, 122, 31, 104, 30, 28, 29, 500, 205, 127, 108, 209, 126, 112, 213, 35, 34, 32, 33, 116, 217, 131, 120, 221, 124, 225, 130, 128, 39, 135, 38, 36, 37, 229, 43, 132, 134, 139, 42, 233, 40, 41, 47, 138, 136, 237, 143, 46, 142, 44, 45, 140, 241, 147, 146, 144, 245,),
+    ),
+  ),
+)
 
 SCRATCH = dict(
     w_qkv=((D, 3 * D), BF16),
@@ -654,27 +770,29 @@
     d_entry=((ROWS, D), F32),
     right=((RIGHTS, ROWS, WIDE), BF16),
     right_in=((RIGHTS, ROWS, WIDE), BF16),
+    left_x=((2, SHARED - 1, 4, PART, ROWS), BF16),
+    right_x=((2, ROWS, WIDE), BF16),
     left=((LEFTS, 8, PART, ROWS), BF16),
     left_out=((LEFTS, 8, PART, ROWS), BF16),
     left_in=((LEFTS, 8, PART, ROWS), BF16),
     grad=((UNITS, 2, 4, PART, WIDE), BF16),
-    ax=((A_UNITS, 4, PART, WIDE), BF16),
-    az=((A_UNITS, 5, PART, WIDE), BF16),
-    bz=((SUM_Z_FIRST, 5, 2, PART, WIDE), BF16),
-    bs=((SUM_Z_FIRST, PART, WIDE), BF16),
-    bx=((SUM_Z_FIRST, PART, WIDE), BF16),
+    ax=((X_UNITS, 4, PART, WIDE), BF16),
+    az=((Z_UNITS, 5, PART, WIDE), BF16),
+    bz=((5, 2, PART, WIDE), BF16),
+    bs=((PART, WIDE), BF16),
+    bx=((PART, WIDE), BF16),
     vec=((8, WIDE), F32),
     vec_in=((5, 8, WIDE), F32),
-    vec_part=((3, 8, WIDE), F32),
+    vec_part=((5, 8, WIDE), F32),
 )
 SEMS = dict(
-    load=(5,), ys=(4,), yr=(4,), ls=(4,), lr=(4,), rs=(4,), rr=(4,),
-    axs=(A_UNITS,), axr=(A_UNITS,), azs=(A_UNITS, 5), azr=(A_UNITS, 5),
-    bzs=(SUM_Z_FIRST, 5), bzr=(SUM_Z_FIRST, 5), bxs=(SUM_Z_FIRST,), bxr=(SUM_Z_FIRST,),
+    load=(5,), ys=(4,), yr=(4,), ls=(4,), lr=(4,), rs=(7,), rr=(7,),
+    axs=(X_UNITS, 4), axr=(X_UNITS, 4), azs=(Z_UNITS, 5), azr=(Z_UNITS, 5),
+    bzs=(5,), bzr=(5,), bxs=(1,), bxr=(1,), gs=(3, 2), gr=(3, 2), lxs=(2,), lxr=(2,),
     vs=(5,), vr=(5,),
 )
 LEFT_GROUPS = ((0, 4), (4, 1), (5, 1), (6, 1))
-RIGHT_GROUPS = ((0, 1), (1, 4), (5, 1), (6, 3))
+RIGHT_GROUPS = (None, (1, 1), (2, 1), (3, 1), (4, 1), (5, 1), (6, 3))
 
 
 def kernel(*refs):
@@ -691,6 +809,7 @@
 
     near_core = dp_of(z, x, 1 - core)
     near_x = dp_of(z, 1 - x, core)
+    diagonal = dp_of(z, 1 - x, 1 - core)
     near_y = (place, 1 - section)
     near_side = dp_of(half * 2 + 1 - z % 2, x, core)
     near_mid = dp_of(3 - z, x, core)
@@ -712,8 +831,7 @@
         pltpu.make_async_copy(src, dst, R.load.at[i])
         for i, (src, dst) in enumerate(zip(weights_in, weights))
     ]
-    for load in loads:
-        load.start()
+    loads[0].start()
 
     def take(index, src, dst):
         @pl.when(section == index)
@@ -729,22 +847,42 @@
     take(1, R.cotangent, R.right.at[0])
 
     barrier = pltpu.get_barrier_semaphore()
-    for device in (near_core, near_x, near_y, near_side):
+    for device in (near_core, near_x, diagonal, near_y, near_side):
         pl.semaphore_signal(barrier, inc=1, device_id=device, device_id_type=MESH)
 
     @pl.when(inner)
     def _():
         pl.semaphore_signal(barrier, inc=1, device_id=near_mid, device_id_type=MESH)
 
+    def all_here():
+        pl.when(inner)(lambda: pl.semaphore_wait(barrier, 6))
+        pl.when(outer)(lambda: pl.semaphore_wait(barrier, 5))
+
     build_tables(R.lengths, R.cos, R.sin, R.mask)
-
-    @pl.when(inner)
+    for load in loads[1:]:
+        load.start()
+
+    def share(kind, m):
+        rows = pl.ds(m * SLOT, SLOT)
+        src, dst, device = (
+            (R.right.at[0, rows], R.right_in.at[0, rows], near_core),
+            (R.right.at[0, rows], R.right_x.at[0, rows], near_x),
+            (R.right_x.at[0, rows], R.right_x.at[1, rows], near_core),
+        )[kind]
+        return copy(src, dst, R.gs.at[kind, m], R.gr.at[kind, m], device)
+
+    def left_x_copy(kind):
+        src, device = ((R.left, near_x), (R.left_out, diagonal))[kind]
+        src = src.at[pl.ds(1, SHARED - 1), pl.ds((1 - x) * 4, 4)]
+        return copy(src, R.left_x.at[kind], R.lxs.at[kind], R.lxr.at[kind], device)
+
+    @pl.when(section == 1)
     def _():
-        pl.semaphore_wait(barrier, 5)
-
-    @pl.when(outer)
-    def _():
-        pl.semaphore_wait(barrier, 4)
+        all_here()
+        pltpu.make_async_copy(R.cotangent, R.right.at[0], R.load.at[4]).wait()
+        for m in range(MICRO):
+            share(0, m).start()
+            share(1, m).start()
 
     def x_copy(m):
         rows = pl.ds(m * SLOT, SLOT)
@@ -757,16 +895,35 @@
         )
 
     taken(0, R.inputs, R.x)
+    @pl.when(section == 0)
+    def _():
+        R.slope[...] = jnp.ones((ROWS, FF), F32)
+
+    @pl.when(section == 1)
+    def _():
+        loads[3].wait()
+        for t in range(FF // 256):
+            cols = pl.ds(t * 256, 256)
+            R.slope[:, cols] = dot_nt(R.right[0], R.w_down[cols, :])
+
     for m in range(MICRO):
 
         @pl.when(section == 1)
         def _():
             x_copy(m).wait_recv()
 
-        forward(R, m, lambda n: loads[n].wait() if m == 0 else None)
+        def arrives(n):
+            if m == 0 and n < 3:
+                loads[n].wait()
+            elif m == 0:
+                pl.when(section == 0)(lambda: loads[3].wait())
+
+        forward(R, m, arrives)
 
         @pl.when(section == 0)
         def _():
+            if m == 0:
+                all_here()
             x_copy(m).start()
 
     def left_copy(i):
@@ -787,14 +944,17 @@
         turn_lefts(R, core)
         for i in range(4):
             left_copy(i).start()
+        for kind in range(2):
+            left_x_copy(kind).start()
 
     @pl.when(section == 0)
     def _():
         send_lefts()
         for m in range(MICRO):
             g_copy(m).wait_recv()
-
-    taken(1, R.cotangent, R.right.at[0])
+            share(0, m).start()
+            share(1, m).start()
+
 
     def weight_unit(u):
         left, right = UNIT_LEFT[u], UNIT_RIGHT[u]
@@ -803,239 +963,300 @@
         total = dot(own, R.right[right]) + dot(other, R.right_in[right])
         R.grad[u] = total.astype(BF16).reshape(2, 4, PART, WIDE)
 
-    def finish(u, total):
-        if u < 4:
-            R.sum_down[u * PART : (u + 1) * PART, :] = total
-        elif u < 8:
-            R.sum_up[:, (u - 4) * WIDE : (u - 3) * WIDE] = total
-        elif u == 8:
-            R.sum_out[...] = total
+    def shared_unit(u):
+        mine = pl.ds(x * 4, 4)
+        factors = (
+            (R.left[u, mine], R.right[0]),
+            (R.left_in[u, mine], R.right_in[0]),
+            (R.left_x[0, u - 1], R.right_x[0]),
+            (R.left_x[1, u - 1], R.right_x[1]),
+        )
+        total = sum(dot(a.reshape(4 * PART, ROWS), b) for a, b in factors)
+        R.grad[u, x] = total.astype(BF16).reshape(4, PART, WIDE)
+
+    def place_of(u):
+        if u < SHARED:
+            return R.sum_down, u * PART, slice(None)
+        if u < 8:
+            return R.sum_up, 0, slice((u - 4) * WIDE, (u - 3) * WIDE)
+        if u == 8:
+            return R.sum_out, 0, slice(None)
+        return R.sum_qkv, 0, slice((u - 9) * WIDE, (u - 8) * WIDE)
+
+    def add_up(terms, ref, at, first=0, columns=slice(None)):
+        def some_rows(r, _):
+            rows = pl.ds(pl.multiple_of(r * 16, 16), 16)
+            total = sum(array[(*index, rows)].astype(F32) for array, index in terms)
+            to = pl.ds(pl.multiple_of(first + r * 16, 16), 16)
+            ref[(*at, to, columns)] = total.astype(ref.dtype)
+            return 0
+
+        lax.fori_loop(0, PART // 16, some_rows, 0)
+
+    def finish(u, terms):
+        ref, first, columns = place_of(u)
+        add_up(terms, ref, (), first, columns)
+
+    def start(make, *operands):
+        make(*operands).start()
+
+    def ax_copy(u, j):
+        i = u - SHARED
+        return copy(
+            R.grad.at[u, 1 - x, owner(j)], R.ax.at[i, j], R.axs.at[i, j], R.axr.at[i, j], near_x
+        )
+
+    def az_copy(u, src, at, slot, device):
+        i = u - 1
+        return copy(src.at[at], R.az.at[i, slot], R.azs.at[i, slot], R.azr.at[i, slot], device)
+
+    def x_sum(u, j):
+        own = (R.grad, (u, x, owner(j)))
+        if u < SHARED:
+            return [own]
+        ax_copy(u, j).wait_recv()
+        return [own, (R.ax, (u - SHARED, j))]
+
+    def x_send(is_outer, u, j):
+        start(ax_copy, u, j)
+
+    def z_send(is_outer, u, j):
+        if is_outer and u < SHARED:
+            start(az_copy, u, R.grad, (u, x, owner(j)), j - 1, near_side)
+            return
+        total = x_sum(u, j)
+        if is_outer:
+            add_up(total, R.ax, (u - SHARED, j))
+            start(az_copy, u, R.ax, (u - SHARED, j), j - 1, near_side)
+            return
+        slot, device = (j - 1, near_side) if j else (3, near_mid)
+        at = (u - 1, slot)
+        az_copy(u, R.az, at, slot, device).wait_recv()
+        add_up(total + [(R.az, at)], R.az, at)
+        if j:
+            start(az_copy, u, R.az, at, 6 - j, near_mid)
         else:
-            R.sum_qkv[:, (u - 9) * WIDE : (u - 8) * WIDE] = total
-
-    started = {}
-
-    def start(condition, make, *operands):
-        started[(condition, make) + operands[:1] + operands[-2:-1]] = (condition, make, operands)
-        make(*operands).start()
-
-    def ax_copy(i):
-        u = i + SUM_Z_FIRST
-        return copy(R.grad.at[u, 1 - x], R.ax.at[i], R.axs.at[i], R.axr.at[i], near_x)
-
-    def az_copy(i, src, at, slot, device):
-        return copy(
-            src.at[at], R.az.at[i, slot], R.azs.at[i, slot], R.azr.at[i, slot], device
-        )
-
-    def a0(i):
-        start(EVERY, ax_copy, i)
-
-    def a1(i):
-        ax_copy(i).wait_recv()
-        for j in range(4):
-            R.ax[i, j] = R.ax[i, j] + R.grad[i + SUM_Z_FIRST, x, j]
-
-        @pl.when(outer)
-        def _():
-            for j in (3, 2, 1):
-                start(OUTER, az_copy, i, R.ax, (i, owner(j)), j - 1, near_side)
-
-    def a2(i):
-        @pl.when(inner)
-        def _():
-            for j in (3, 2):
-                az_copy(i, R.az, (i, j - 1), j - 1, near_side).wait_recv()
-                R.az[i, j - 1] = R.az[i, j - 1] + R.ax[i, owner(j)]
-                start(INNER, az_copy, i, R.az, (i, j - 1), 6 - j, near_mid)
-
-    def a3(i):
-        @pl.when(inner)
-        def _():
-            az_copy(i, R.az, (i, 3), 3, near_mid).wait_recv()
-            R.az[i, 3] = R.az[i, 3] + R.ax[i, owner(0)]
-            start(INNER, az_copy, i, R.az, (i, 3), 0, near_side)
-
-    def a4(i):
-        u = i + SUM_Z_FIRST
-
-        @pl.when(inner)
-        def _():
-            az_copy(i, R.az, (i, 0), 0, near_side).wait_recv()
-            az_copy(i, R.az, (i, 4), 4, near_mid).wait_recv()
-            finish(
-                u,
-                R.ax[i, owner(1)].astype(F32)
-                + R.az[i, 0].astype(F32)
-                + R.az[i, 4].astype(F32),
-            )
-
-        @pl.when(outer)
-        def _():
-            az_copy(i, R.az, (i, 0), 0, near_side).wait_recv()
-            finish(u, R.ax[i, owner(0)].astype(F32) + R.az[i, 0].astype(F32))
-
-    def bz_copy(i, src, at, slot, device):
-        return copy(
-            src.at[at], R.bz.at[i, slot], R.bzs.at[i, slot], R.bzr.at[i, slot], device
-        )
-
-    def bx_copy(i):
-        return copy(R.bs.at[i], R.bx.at[i], R.bxs.at[i], R.bxr.at[i], near_x)
-
-    def b0(i):
-        @pl.when(outer)
-        def _():
-            for j in (3, 2, 1):
-                start(OUTER, bz_copy, i, R.grad, (i, slice(None), owner(j)), j - 1, near_side)
-
-    def b1(i):
-        @pl.when(inner)
-        def _():
-            for j in (3, 2):
-                bz_copy(i, R.bz, (i, j - 1), j - 1, near_side).wait_recv()
-                for a in range(2):
-                    R.bz[i, j - 1, a] = R.bz[i, j - 1, a] + R.grad[i, a, owner(j)]
-                start(INNER, bz_copy, i, R.bz, (i, j - 1), 6 - j, near_mid)
-
-    def b2(i):
-        @pl.when(inner)
-        def _():
-            bz_copy(i, R.bz, (i, 3), 3, near_mid).wait_recv()
-            for a in range(2):
-                R.bz[i, 3, a] = R.bz[i, 3, a] + R.grad[i, a, owner(0)]
-            start(INNER, bz_copy, i, R.bz, (i, 3), 0, near_side)
-
-    def b_total(i, a):
-        own = R.grad[i, a, z].astype(F32) + R.bz[i, 0, a].astype(F32)
-        return own
-
-    def b3(i):
-        @pl.when(inner)
-        def _():
-            bz_copy(i, R.bz, (i, 0), 0, near_side).wait_recv()
-            bz_copy(i, R.bz, (i, 4), 4, near_mid).wait_recv()
-            R.bs[i] = (b_total(i, 1 - x) + R.bz[i, 4, 1 - x].astype(F32)).astype(BF16)
-
-        @pl.when(outer)
-        def _():
-            bz_copy(i, R.bz, (i, 0), 0, near_side).wait_recv()
-            R.bs[i] = b_total(i, 1 - x).astype(BF16)
-
-        start(EVERY, bx_copy, i)
-
-    def b4(i):
-        bx_copy(i).wait_recv()
-
-        @pl.when(inner)
-        def _():
-            finish(i, b_total(i, x) + R.bz[i, 4, x].astype(F32) + R.bx[i].astype(F32))
-
-        @pl.when(outer)
-        def _():
-            finish(i, b_total(i, x) + R.bx[i].astype(F32))
+            start(az_copy, u, R.az, at, 0, near_side)
+
+    def z_last(is_outer, u, j):
+        total = x_sum(u, j)
+        for slot, device in ((0, near_side),) if is_outer else ((0, near_side), (4, near_mid)):
+            az_copy(u, R.az, (u - 1, slot), slot, device).wait_recv()
+            total.append((R.az, (u - 1, slot)))
+        finish(u, total)
+
+    def bz_copy(src, at, slot, device):
+        return copy(src.at[at], R.bz.at[slot], R.bzs.at[slot], R.bzr.at[slot], device)
+
+    def bx_copy():
+        return copy(R.bs, R.bx, R.bxs.at[0], R.bxr.at[0], near_x)
+
+    def bz_send(is_outer, u, j):
+        if is_outer:
+            start(bz_copy, R.grad, (0, slice(None), owner(j)), j - 1, near_side)
+            return
+        slot, device = (j - 1, near_side) if j else (3, near_mid)
+        bz_copy(R.bz, slot, slot, device).wait_recv()
+        for a in range(2):
+            add_up([(R.bz, (slot, a)), (R.grad, (0, a, owner(j)))], R.bz, (slot, a))
+        if j:
+            start(bz_copy, R.bz, slot, 6 - j, near_mid)
+        else:
+            start(bz_copy, R.bz, slot, 0, near_side)
+
+    def b_total(is_outer, a):
+        terms = [(R.grad, (0, a, z)), (R.bz, (0, a)), (R.bz, (4, a))]
+        return terms[:2] if is_outer else terms
+
+    def bx_send(is_outer, u, j):
+        bz_copy(R.bz, 0, 0, near_side).wait_recv()
+        if not is_outer:
+            bz_copy(R.bz, 4, 4, near_mid).wait_recv()
+        add_up(b_total(is_outer, 1 - x), R.bs, ())
+        start(bx_copy)
+
+    def bx_last(is_outer, u, j):
+        bx_copy().wait_recv()
+        finish(0, b_total(is_outer, x) + [(R.bx, ())])
 
     def v_copy(stage, src, at, device):
         return copy(src.at[at] if at is not None else src, R.vec_in.at[stage], R.vs.at[stage], R.vr.at[stage], device)
 
-    def v0():
-        start(EVERY, v_copy, 0, R.vec, None, near_core)
-
-    def v1():
-        v_copy(0, R.vec, None, near_core).wait_recv()
-        R.vec_part[0] = R.vec[...] + R.vec_in[0]
-        start(EVERY, v_copy, 1, R.vec_part, 0, near_x)
-
-    def v2():
-        v_copy(1, R.vec_part, 0, near_x).wait_recv()
-        R.vec_part[1] = R.vec_part[0] + R.vec_in[1]
-
-        @pl.when(outer)
-        def _():
-            start(OUTER, v_copy, 2, R.vec_part, 1, near_side)
-
-    def v3():
-        @pl.when(inner)
-        def _():
+    def v_step(is_outer, high, low):
+        stage = 4 * high + low
+        if stage == 0:
+            R.vec_part[3] = R.vec[...]
+            start(v_copy, 0, R.vec_part, 3, near_core)
+        elif stage == 1:
+            v_copy(0, R.vec_part, 3, near_core).wait_recv()
+            R.vec_part[0] = R.vec[...] + R.vec_in[0]
+            start(v_copy, 1, R.vec_part, 0, near_x)
+        elif stage == 2:
+            v_copy(1, R.vec_part, 0, near_x).wait_recv()
+            R.vec_part[1] = R.vec_part[0] + R.vec_in[1]
+            if is_outer:
+                start(v_copy, 2, R.vec_part, 1, near_side)
+        elif stage == 3:
             v_copy(2, R.vec_part, 1, near_side).wait_recv()
             R.vec_part[2] = R.vec_part[1] + R.vec_in[2]
-            start(INNER, v_copy, 3, R.vec_part, 2, near_mid)
-
-    def v4():
-        @pl.when(inner)
+            start(v_copy, 3, R.vec_part, 2, near_mid)
+        elif stage == 4:
+            v_copy(3, R.vec_part, 2, near_mid).wait_recv()
+            R.vec_part[4] = R.vec_part[2] + R.vec_in[3]
+            R.vec_sum[...] = R.vec_part[4]
+            start(v_copy, 4, R.vec_part, 4, near_side)
+        else:
+            v_copy(4, R.vec_part, 3, near_side).wait_recv()
+            R.vec_sum[...] = R.vec_in[4]
+
+    steps = (x_send, z_send, z_last, bz_send, bx_send, bx_last, v_step)
+
+    def serve(which, step):
+        def run(is_outer, codes):
+            for code in codes:
+                kind, rest = divmod(code, 100)
+                steps[kind](is_outer, rest // 4, rest % 4)
+
+        codes_outer, codes_inner = (order[step] for order in ORDER[which])
+        if codes_outer:
+            pl.when(outer)(lambda: run(True, codes_outer))
+        if codes_inner:
+            pl.when(inner)(lambda: run(False, codes_inner))
+
+    done = [0]
+
+    def between(*more):
+        @pl.when(section == 0)
         def _():
-            v_copy(3, R.vec_part, 2, near_mid).wait_recv()
-            R.vec_sum[...] = R.vec_part[2] + R.vec_in[3]
-            start(INNER, v_copy, 4, R.vec_sum, None, near_side)
-
-    def v5():
-        @pl.when(outer)
-        def _():
-            v_copy(4, R.vec_part, 2, near_side).wait_recv()
-            R.vec_sum[...] = R.vec_in[4]
-
-    def first_units():
+            for item in more or (None,):
+                serve(0, done[0])
+                done[0] += 1
+                if item is not None:
+                    item()
+
+    def unit(u):
+        return lambda: weight_unit(u)
+
+    def shared_arrives(m):
+        share(1, m).wait_recv()
+        share(2, m).start()
+
+    @pl.when(section == 1)
+    def _():
+        for m in range(MICRO):
+            shared_arrives(m)
+
+    R.vec[...] = jnp.zeros((8, WIDE), F32)
+
+    @pl.when(section == 0)
+    def _():
         left_copy(0).wait_recv()
-        right_copy(0).wait_recv()
-        for u, send, i in ((0, b0, 0), (2, a0, 0), (1, b0, 1), (3, a0, 1)):
-            weight_unit(u)
-            send(i)
-
-    right_copy(0).start()
-    R.vec[...] = jnp.zeros((8, WIDE), F32)
-    pl.when(section == 0)(first_units)
-    backward_feed(R)
-    right_copy(1).start()
-    right_copy(2).start()
+        for m in range(MICRO):
+            share(0, m).wait_recv()
+        shared_arrives(0)
+
+    def unit_up(i):
+        def run():
+            if i == 0:
+                left_copy(1).wait_recv()
+            right_copy(1 + i).wait_recv()
+            weight_unit(SHARED + i)
+
+        return run
+
+    between(unit(0))
+    for t in range(4):
+        between()
+        pl.when(section == 0)(lambda: feed_inner_matmul(R, t))
+        feed_inner(R, t)
+        right_copy(1 + t).start()
+    for t in range(3):
+        between()
+        feed_entry(R, t)
+    between()
+    feed_norm(R)
+    right_copy(5).start()
+    between(*[unit_up(i) for i in range(4)])
+    between()
+    attention_mixed(R)
+
+    def shared_units():
+        for kind in range(2):
+            left_x_copy(kind).wait_recv()
+        for m in range(MICRO):
+            share(2, m).wait_recv()
+
     for m in range(MICRO):
-        backward_attention(R, m)
+        for t in range(3):
+            between()
+            attention_pairs(R, m, t)
+            if m == 0 and t == 0:
+                pl.when(section == 0)(lambda: shared_arrives(1))
+        between()
+        attention_entry(R, m)
+        if m == 0:
+            pl.when(section == 0)(shared_units)
+            between(*[lambda u=u: shared_unit(u) for u in range(1, SHARED)])
 
         @pl.when(section == 1)
         def _():
             g_copy(m).start()
 
-    right_copy(3).start()
+    right_copy(6).start()
+
+    @pl.when(section == 0)
+    def _():
+        for i in (2, 3):
+            left_copy(i).wait_recv()
+            right_copy(3 + i).wait_recv()
+
+    between(*[unit(u) for u in range(8, UNITS)])
+    pl.when(section == 0)(lambda: serve(0, done[0]))
 
     @pl.when(section == 1)
     def _():
         send_lefts()
-        first_units()
-
-    for i in range(1, 4):
-        left_copy(i).wait_recv()
-        right_copy(i).wait_recv()
-
-    events = []
-    for u in range(4, UNITS):
-        i = u - SUM_Z_FIRST
-        events += [(0.0, weight_unit, u)]
-        if i < DEPTH:
-            events += [(0.0, a0, i)]
-    for i, t in enumerate((7.0, 16.0)):
-        events += [(t, b1, i), (t + 4, b2, i), (t + 8, b3, i), (t + 12, b4, i)]
-    for i in range(A_UNITS):
-        t1 = 6.4 * (i + 1)
-        t2 = max(t1 + 6.0, 20.0 + 4.7 * (i + 1))
-        events += [(t1, a1, i), (t2, a2, i), (t2 + 3.5, a3, i), (t2 + 7.0, a4, i)]
-        if i + DEPTH < A_UNITS:
-            events += [(t1, a0, i + DEPTH)]
-    for i, step in enumerate((v0, v1, v2, v3, v4, v5)):
-        events += [(20.0 + 4.0 * i, step, None)]
-    for _, step, index in sorted(events, key=lambda e: e[0]):
-        step() if index is None else step(index)
+        left_copy(0).wait_recv()
+        for m in range(MICRO):
+            share(0, m).wait_recv()
+        for i in range(1, 4):
+            left_copy(i).wait_recv()
+        for i in range(1, 7):
+            right_copy(i).wait_recv()
+        for step, u in enumerate((0,) + tuple(range(4, UNITS)) + (1, 2, 3)):
+            serve(1, step)
+            if u == 1:
+                shared_units()
+            if 0 < u < SHARED:
+                shared_unit(u)
+            else:
+                weight_unit(u)
+        serve(1, UNITS)
 
     for i in range(4):
         left_copy(i).wait_send()
+    for i in range(1, 7):
         right_copy(i).wait_send()
-
-    def wait_sent(name):
-        for condition, make, operands in started.values():
-            if condition == name:
-                make(*operands).wait_send()
-
-    wait_sent(EVERY)
-    pl.when(inner)(lambda: wait_sent(INNER))
-    pl.when(outer)(lambda: wait_sent(OUTER))
+    for kind in range(2):
+        left_x_copy(kind).wait_send()
+    for kind in range(3):
+        for m in range(MICRO):
+            share(kind, m).wait_send()
+
+    def every_sent(is_outer):
+        for u in range(SHARED, UNITS):
+            for j in range(4):
+                ax_copy(u, j).wait_send()
+        for slot in (0, 1, 2) if is_outer else (3, 4, 0):
+            for u in range(1, UNITS):
+                az_copy(u, R.az, (u - 1, slot), slot, near_side).wait_send()
+            bz_copy(R.bz, slot, slot, near_side).wait_send()
+        bx_copy().wait_send()
+        for stage in (0, 1, 2) if is_outer else (0, 1, 3, 4):
+            v_copy(stage, R.vec_part, 0, near_side).wait_send()
+
+    pl.when(outer)(lambda: every_sent(True))
+    pl.when(inner)(lambda: every_sent(False))
 
     for m in range(MICRO):
 

time: 142 us -> 124 us (0.87)
  Pallas kernels: 140 us -> 123 us
    pallas_call x1, Pallas kernels: 137 us -> 119 us  [layer_device(): pl.pallas_call(kernel, out_shape=[jax.ShapeDtypeStruct(s, d) for s, d in...]
where the time goes in v2:
time: 124 us
  Pallas kernels  123 us (99%)
    pallas_call x1, Pallas kernels, layer_device(): pl.pallas_call(kernel, out_shape=[jax.ShapeDtypeStruct(s, d) for s, d in...  119 us
    pallas_call x1, Pallas kernels, layer_device(): pl.pallas_call(settle, out_shape=[jax.ShapeDtypeStruct((1, PART), F32), j...  3.78 us

profile of v2, /device:TPU:0, one launch (start us, length us, event | category | flops | bytes accessed | tf_op | source)
XLA Modules:
  0.0 123.9 jit_solution(15795114172841268965)
XLA Ops:
  0.6 119.3 %layers.1 = (bf16[256,768]{1,0:T(8,128)(2,1)}, bf16[256,768]{1,0:T(8,128)(2,1)}, f32[48,2304]{1,0:T(8,128)}, f32[48,768]{1,0:T(8,128)}, f32[48,3072]{1,0:T(8,128...) custom-call(bf16[256,768]{1,0:T(8,128)(2,1)} %bitcast.17, bf16[256,768]{1,0:T(8,128)(2,1)} %bitcast.18, s32[2,3]{1,0:T(2,128)} %bitcast.19, ...), custom_call_target="tpu_custom_call" | custom-call | tf_op jit(solution)/shard_map/layers/pallas_call | solution.py:1292
  120.0 3.8 %settle.1 = (f32[1,48]{1,0:T(1,128)}, f32[1,48]{1,0:T(1,128)}, f32[1,48]{1,0:T(1,128)}, f32[1,192]{1,0:T(1,128)}, bf16[256,768]{1,0:T(8,128)(2,1)}, /*index=5*/b...) custom-call(f32[8,768]{1,0:T(8,128)} %get-tuple-element.27.vec, ...), custom_call_target="tpu_custom_call" | custom-call | tf_op jit(solution)/shard_map/settle/pallas_call | solution.py:1307

commit v3 on v2

--- a/solution.py
+++ b/solution.py
@@ -23,6 +23,7 @@
 BF16 = jnp.bfloat16
 MESH = pl.DeviceIdType.MESH
 MICRO = 2
+BLOCK_BITS = BLOCK.bit_length() - 1
 SLOT = 2 * SEQ_TOK
 ROWS = MICRO * SLOT
 PAIRS = HEADS // 2
@@ -87,13 +88,26 @@
 
 
 def build_tables(lengths, cos_t, sin_t, mask_t):
+    half = HEAD_DIM // 2
     for m in range(MICRO):
         first, second = lengths[m, 0], lengths[m, 1]
+        row = lax.broadcasted_iota(jnp.int32, (SEQ_TOK, LANES), 0)
+        col = lax.broadcasted_iota(jnp.int32, (SEQ_TOK, LANES), 1)
+        _, position = token_tables(row, first, second)
+        frequency = jnp.exp((col & (half - 1)).astype(F32) * (-2.0 * math.log(10000.0) / HEAD_DIM))
+        angle = position.astype(F32) * frequency
+        both = jnp.sin(jnp.where(col < HEAD_DIM, angle + math.pi / 2, angle))
+        other = pltpu.roll(both, HEAD_DIM, 1)
+        cosine = jnp.where(col < HEAD_DIM, both, other)
+        sine = jnp.where(col < HEAD_DIM, other, both)
+        sine = jnp.where((col & (HEAD_DIM - 1)) < half, -sine, sine)
+        cos_t[m] = jnp.concatenate([cosine, cosine], axis=0)
+        sin_t[m] = jnp.concatenate([sine, sine], axis=0)
         row = lax.broadcasted_iota(jnp.int32, (SLOT, LANES), 0)
         col = lax.broadcasted_iota(jnp.int32, (SLOT, LANES), 1)
-        doc_r, pos_r = token_tables(row % SEQ_TOK, first, second)
-        doc_c, pos_c = token_tables(col % SEQ_TOK, first, second)
-        block_r, block_c = pos_r // BLOCK, pos_c // BLOCK
+        doc_r, pos_r = token_tables(row & (SEQ_TOK - 1), first, second)
+        doc_c, pos_c = token_tables(col & (SEQ_TOK - 1), first, second)
+        block_r, block_c = pos_r >> BLOCK_BITS, pos_c >> BLOCK_BITS
         noisy_r, noisy_c = row < SEQ_TOK, col < SEQ_TOK
         same = (doc_r == doc_c) & (doc_r < SEGS - 1)
         ruling = (noisy_r & noisy_c & (block_r == block_c)) | (
@@ -105,12 +119,6 @@
         )
         allowed = (same & ruling) | (row == col)
         mask_t[m] = jnp.where(allowed, 1.0, 0.0)
-        half = HEAD_DIM // 2
-        frequency = jnp.exp((col % half).astype(F32) * (-2.0 * math.log(10000.0) / HEAD_DIM))
-        angle = pos_r.astype(F32) * frequency
-        sign = jnp.where((col % HEAD_DIM) < half, -1.0, 1.0)
-        cos_t[m] = jnp.cos(angle)
-        sin_t[m] = jnp.sin(angle) * sign
 
 
 def rotate_pair(values, cosine, sine):
@@ -255,7 +263,7 @@
     ).astype(BF16)
 
 
-def turn_lefts(R, core):
+def turn_lefts(R, core, group):
     def place(kind, owner_core, chip, block):
         x, z = chip % 2, chip // 2
 
@@ -267,10 +275,11 @@
         def _():
             R.left_out[kind, x * 4 + z] = block
 
-    for kind, factor in ((4, R.entry2), (5, R.mixed), (6, R.entry)):
-        turned = factor[...].T
+    if group:
+        turned = (R.entry2, R.mixed, R.entry)[group - 1][...].T
         for d in range(16):
-            place(kind, d % 2, d // 2, turned[d * PART : (d + 1) * PART, :])
+            place(3 + group, d % 2, d // 2, turned[d * PART : (d + 1) * PART, :])
+        return
     for d4 in range(4):
         turned = R.act[:, d4 * 768 : (d4 + 1) * 768].T
         for e in range(4):
@@ -631,8 +640,8 @@
     gain_b=VMEM, w_up_in=ANY, b_up=VMEM, w_down_in=ANY, b_down=VMEM,
 )
 OUT = dict(
-    y=((ROWS, D), BF16),
-    d_state=((ROWS, D), BF16),
+    y_out=((ROWS, D), BF16),
+    d_state_out=((ROWS, D), BF16),
     sum_qkv=((PART, 3 * D), F32),
     sum_out=((PART, D), F32),
     sum_up=((PART, FF), F32),
@@ -749,6 +758,8 @@
     w_up=((D, FF), BF16),
     w_down=((FF, D), BF16),
     x=((ROWS, D), BF16),
+    y=((ROWS, D), BF16),
+    d_state=((ROWS, D), BF16),
     cos=((MICRO, SLOT, LANES), F32),
     sin=((MICRO, SLOT, LANES), F32),
     mask=((MICRO, SLOT, SLOT), F32),
@@ -786,7 +797,7 @@
     vec_part=((5, 8, WIDE), F32),
 )
 SEMS = dict(
-    load=(5,), ys=(4,), yr=(4,), ls=(4,), lr=(4,), rs=(7,), rr=(7,),
+    load=(7,), ys=(4,), yr=(4,), ls=(4,), lr=(4,), rs=(7,), rr=(7,),
     axs=(X_UNITS, 4), axr=(X_UNITS, 4), azs=(Z_UNITS, 5), azr=(Z_UNITS, 5),
     bzs=(5,), bzr=(5,), bxs=(1,), bxr=(1,), gs=(3, 2), gr=(3, 2), lxs=(2,), lxr=(2,),
     vs=(5,), vr=(5,),
@@ -926,6 +937,12 @@
                 all_here()
             x_copy(m).start()
 
+    leaves = (
+        pltpu.make_async_copy(R.y, R.y_out, R.load.at[5]),
+        pltpu.make_async_copy(R.d_state, R.d_state_out, R.load.at[6]),
+    )
+    leaves[0].start()
+
     def left_copy(i):
         a, n = LEFT_GROUPS[i]
         rows = pl.ds(a, n)
@@ -940,16 +957,17 @@
             R.right.at[rows], R.right_in.at[rows], R.rs.at[i], R.rr.at[i], near_core
         )
 
-    def send_lefts():
-        turn_lefts(R, core)
-        for i in range(4):
-            left_copy(i).start()
-        for kind in range(2):
-            left_x_copy(kind).start()
+    def send_lefts(groups):
+        for group in groups:
+            turn_lefts(R, core, group)
+            left_copy(group).start()
+        if 1 in groups:
+            for kind in range(2):
+                left_x_copy(kind).start()
 
     @pl.when(section == 0)
     def _():
-        send_lefts()
+        send_lefts(range(4))
         for m in range(MICRO):
             g_copy(m).wait_recv()
             share(0, m).start()
@@ -1203,6 +1221,7 @@
             g_copy(m).start()
 
     right_copy(6).start()
+    leaves[1].start()
 
     @pl.when(section == 0)
     def _():
@@ -1215,16 +1234,18 @@
 
     @pl.when(section == 1)
     def _():
-        send_lefts()
+        send_lefts(range(2))
         left_copy(0).wait_recv()
         for m in range(MICRO):
             share(0, m).wait_recv()
-        for i in range(1, 4):
-            left_copy(i).wait_recv()
-        for i in range(1, 7):
-            right_copy(i).wait_recv()
         for step, u in enumerate((0,) + tuple(range(4, UNITS)) + (1, 2, 3)):
             serve(1, step)
+            if step == 1:
+                send_lefts(range(2, 4))
+                for i in range(1, 4):
+                    left_copy(i).wait_recv()
+                for i in range(1, 7):
+                    right_copy(i).wait_recv()
             if u == 1:
                 shared_units()
             if 0 < u < SHARED:
@@ -1233,6 +1254,8 @@
                 weight_unit(u)
         serve(1, UNITS)
 
+    for leave in leaves:
+        leave.wait()
     for i in range(4):
         left_copy(i).wait_send()
     for i in range(1, 7):
@@ -1270,9 +1293,13 @@
 
 
 def settle(vec, *refs):
-    arrays, narrow, wide, sems = refs[:6], refs[6:10], refs[10:16], refs[16]
-    copies = [pltpu.make_async_copy(a, w, sems.at[i]) for i, (a, w) in enumerate(zip(arrays, wide))]
-    for item in copies:
+    arrays, narrow, wide, held, sems = refs[:6], refs[6:10], refs[10:16], refs[16:22], refs[22]
+    inward = [pltpu.make_async_copy(a, h, sems.at[0, i]) for i, (a, h) in enumerate(zip(arrays, held))]
+    copies = [pltpu.make_async_copy(h, w, sems.at[1, i]) for i, (h, w) in enumerate(zip(held, wide))]
+    for item in inward:
+        item.start()
+    for there, item in zip(inward, copies):
+        there.wait()
         item.start()
     place = lax.axis_index("dp")
     near = pltpu.roll(vec[...], (16 - place) % 16 * PART, 1)
@@ -1293,7 +1320,7 @@
         kernel,
         out_shape=[jax.ShapeDtypeStruct(s, d) for s, d in OUT.values()],
         in_specs=list(IN.values()),
-        out_specs=[VMEM] * len(OUT),
+        out_specs=[ANY] * 2 + [VMEM] * (len(OUT) - 2),
         scratch_shapes=[pltpu.VMEM(s, d) for s, d in SCRATCH.values()]
         + [pltpu.SemaphoreType.DMA(s) for s in SEMS.values()],
         compiler_params=pltpu.CompilerParams(
@@ -1313,9 +1340,10 @@
             jax.ShapeDtypeStruct((1, 4 * PART), F32),
         ]
         + [jax.ShapeDtypeStruct(s, d) for s, d in list(OUT.values())[:6]],
-        in_specs=[VMEM] * 7,
+        in_specs=[VMEM] + [ANY] * 6,
         out_specs=[VMEM] * 4 + [ANY] * 6,
-        scratch_shapes=[pltpu.SemaphoreType.DMA((6,))],
+        scratch_shapes=[pltpu.VMEM(s, d) for s, d in list(OUT.values())[:6]]
+        + [pltpu.SemaphoreType.DMA((2, 6))],
         name="settle",
     )(vec, y, d_state, qkv, out, up, down)
     gain_a, gain_b, bias_down, bias_up, y, d_state, qkv, out, up, down = totals

time: 124 us -> 124 us (level)
  no operation moved by 1% of the time
where the time goes in v3:
time: 124 us
  Pallas kernels  123 us (99%)
    pallas_call x1, Pallas kernels, layer_device(): pl.pallas_call(kernel, out_shape=[jax.ShapeDtypeStruct(s, d) for s, d in...  119 us
    pallas_call x1, Pallas kernels, layer_device(): pl.pallas_call(settle, out_shape=[jax.ShapeDtypeStruct((1, PART), F32), j...  3.91 us

profile of v3, /device:TPU:0, one launch (start us, length us, event | category | flops | bytes accessed | tf_op | source)
XLA Modules:
  0.0 123.9 jit_solution(11431435749656584902)
XLA Ops:
  0.6 119.1 %layers.1 = (bf16[256,768]{1,0:T(8,128)(2,1)}, bf16[256,768]{1,0:T(8,128)(2,1)}, f32[48,2304]{1,0:T(8,128)}, f32[48,768]{1,0:T(8,128)}, f32[48,3072]{1,0:T(8,128...) custom-call(bf16[256,768]{1,0:T(8,128)(2,1)} %bitcast.17, bf16[256,768]{1,0:T(8,128)(2,1)} %bitcast.18, s32[2,3]{1,0:T(2,128)} %bitcast.19, ...), custom_call_target="tpu_custom_call" | custom-call | tf_op jit(solution)/shard_map/layers/pallas_call | solution.py:1319
  119.8 3.9 %settle.1 = (f32[1,48]{1,0:T(1,128)}, f32[1,48]{1,0:T(1,128)}, f32[1,48]{1,0:T(1,128)}, f32[1,192]{1,0:T(1,128)}, bf16[256,768]{1,0:T(8,128)(2,1)}, /*index=5*/b...) custom-call(f32[8,768]{1,0:T(8,128)} %get-tuple-element.27.vec, ...), custom_call_target="tpu_custom_call" | custom-call | tf_op jit(solution)/shard_map/settle/pallas_call | solution.py:1334

commit v4 on v3

--- a/solution.py
+++ b/solution.py
@@ -870,8 +870,11 @@
         pl.when(outer)(lambda: pl.semaphore_wait(barrier, 5))
 
     build_tables(R.lengths, R.cos, R.sin, R.mask)
-    for load in loads[1:]:
-        load.start()
+    def load_rest():
+        for load in loads[1:]:
+            load.start()
+
+    pl.when(section == 1)(load_rest)
 
     def share(kind, m):
         rows = pl.ds(m * SLOT, SLOT)
@@ -926,6 +929,8 @@
         def arrives(n):
             if m == 0 and n < 3:
                 loads[n].wait()
+                if n == 0:
+                    pl.when(section == 0)(load_rest)
             elif m == 0:
                 pl.when(section == 0)(lambda: loads[3].wait())
 

time: 124 us -> 125 us (level)
  no operation moved by 1% of the time
where the time goes in v4:
time: 125 us; the launch traced here: 124 us
  Pallas kernels  123 us (98%)
    pallas_call x1, Pallas kernels, layer_device(): pl.pallas_call(kernel, out_shape=[jax.ShapeDtypeStruct(s, d) for s, d in...  120 us
    pallas_call x1, Pallas kernels, layer_device(): pl.pallas_call(settle, out_shape=[jax.ShapeDtypeStruct((1, PART), F32), j...  3.91 us

profile of v4, /device:TPU:0, one launch (start us, length us, event | category | flops | bytes accessed | tf_op | source)
XLA Modules:
  0.0 124.3 jit_solution(7506956076771409922)
XLA Ops:
  0.6 119.5 %layers.1 = (bf16[256,768]{1,0:T(8,128)(2,1)}, bf16[256,768]{1,0:T(8,128)(2,1)}, f32[48,2304]{1,0:T(8,128)}, f32[48,768]{1,0:T(8,128)}, f32[48,3072]{1,0:T(8,128...) custom-call(bf16[256,768]{1,0:T(8,128)(2,1)} %bitcast.17, bf16[256,768]{1,0:T(8,128)(2,1)} %bitcast.18, s32[2,3]{1,0:T(2,128)} %bitcast.19, ...), custom_call_target="tpu_custom_call" | custom-call | tf_op jit(solution)/shard_map/layers/pallas_call | solution.py:1324
  120.2 3.9 %settle.1 = (f32[1,48]{1,0:T(1,128)}, f32[1,48]{1,0:T(1,128)}, f32[1,48]{1,0:T(1,128)}, f32[1,192]{1,0:T(1,128)}, bf16[256,768]{1,0:T(8,128)(2,1)}, /*index=5*/b...) custom-call(f32[8,768]{1,0:T(8,128)} %get-tuple-element.27.vec, ...), custom_call_target="tpu_custom_call" | custom-call | tf_op jit(solution)/shard_map/settle/pallas_call | solution.py:1339
